TPU v7x, 128 devices: a whole 4x4x4 slice. The times are simulated.
128 devices in a mesh: row: 16 (over y_hi, z, core), col: 4 (over x), rep: 2 (over y_lo).
Axes of the slice: x: 4, y: 4 (y_hi: 2, y_lo: 2; y = y_hi * 2 + y_lo), z: 4, core: 2. Of those that a mesh axis runs over, the one named last changes fastest.
Arguments:
- activations: bfloat16 [2, 2048, 8192], P('rep', 'row', 'col'), may hold values from -6 to 6
- out_grads: bfloat16 [2, 2048, 26624], P('rep', 'col', 'row'), may hold values from -0.1875 to 0.1875
- weight_code: bfloat16 [8192, 26624], P(('col', 'rep'), 'row'), may hold values from -1 to 1
- weight_scale: float32 [64, 208], P(('col', 'rep'), 'row'), may hold values from 0.005 to 0.05
- moment_code: bfloat16 [8192, 26624], P(('col', 'rep'), 'row'), may hold values from -1 to 1
- moment_scale: float32 [64, 208], P(('col', 'rep'), 'row'), may hold values from 0.05 to 0.5
- second_code: bfloat16 [8192, 26624], P(('col', 'rep'), 'row'), may hold values from 0.049804688 to 1
- second_scale: float32 [64, 208], P(('col', 'rep'), 'row'), may hold values from 0.05 to 1
Outputs:
- new_weight: bfloat16 [8192, 26624], P('col', 'row')
- new_weight_scale: float32 [64, 208], P('col', 'row')
- new_moment: bfloat16 [8192, 26624], P(('col', 'rep'), 'row')
- new_moment_scale: float32 [64, 208], P(('col', 'rep'), 'row')
- new_second: bfloat16 [8192, 26624], P(('col', 'rep'), 'row')
- new_second_scale: float32 [64, 208], P(('col', 'rep'), 'row')
All inputs are finite; a program needn't handle non-finite values. Where the computation divides by a largest or mean magnitude, that divisor is 1e-20 or more.
Results may differ from a plain program's by a relative error of at most 0.0095.
Values may be sent and summed in bfloat16 or wider, within the bound.
A program may use at most 192 MiB of HBM per device.

v0:
```python
import jax
import jax.numpy as jnp
from jax import lax
from jax.sharding import PartitionSpec as P


def dequantize(codes, scales):
    rows, cols = codes.shape
    blocks = codes.astype(jnp.float32).reshape(rows // 128, 128, cols // 128, 128)
    return (blocks * scales[:, None, :, None]).reshape(rows, cols)


def quantize(values):
    rows, cols = values.shape
    blocks = values.reshape(rows // 128, 128, cols // 128, 128)
    scales = jnp.max(jnp.abs(blocks), axis=(1, 3)) + 1e-06
    codes = (blocks / scales[:, None, :, None]).reshape(rows, cols).astype(jnp.bfloat16)
    return (codes, scales)


def contract_tokens(left, right):
    return lax.dot_general(
        left, right, (((0,), (0,)), ((), ())), preferred_element_type=jnp.float32
    )


def per_device(
    activations,
    out_grads,
    weight_code,
    weight_scale,
    moment_code,
    moment_scale,
    second_code,
    second_scale,
):
    gathered = lax.all_gather(activations, "row", axis=1, tiled=True)[0]
    partial_value = contract_tokens(
        gathered, lax.all_gather(out_grads, "col", axis=1, tiled=True)[0]
    )
    gradient = lax.psum_scatter(partial_value, "rep", scatter_dimension=0, tiled=True)
    weight = dequantize(weight_code, weight_scale)
    moment = dequantize(moment_code, moment_scale)
    second = dequantize(second_code, second_scale)
    moment1 = 0.9 * moment + 0.1 * gradient
    second1 = 0.95 * second + 0.05 * gradient * gradient
    bias_one = 1.0 - 0.9**10
    bias_two = 1.0 - 0.95**10
    update = moment1 / bias_one / (jnp.sqrt(second1 / bias_two) + 1e-08) + 0.1 * weight
    weight1 = weight - 0.01 * update
    codes_w, scales_w = quantize(weight1)
    codes_m, scales_m = quantize(moment1)
    codes_v, scales_v = quantize(second1)
    full_codes, full_scales = (
        lax.all_gather(codes_w, "rep", axis=0, tiled=True),
        lax.all_gather(scales_w.astype(jnp.bfloat16), "rep", axis=0, tiled=True).astype(
            scales_w.dtype
        ),
    )
    return (full_codes, full_scales, codes_m, scales_m, codes_v, scales_v)


def solution(mesh):
    return jax.shard_map(
        per_device,
        mesh=mesh,
        in_specs=(
            P("rep", "row", "col"),
            P("rep", "col", "row"),
            P(("col", "rep"), "row"),
            P(("col", "rep"), "row"),
            P(("col", "rep"), "row"),
            P(("col", "rep"), "row"),
            P(("col", "rep"), "row"),
            P(("col", "rep"), "row"),
        ),
        out_specs=(
            P("col", "row"),
            P("col", "row"),
            P(("col", "rep"), "row"),
            P(("col", "rep"), "row"),
            P(("col", "rep"), "row"),
            P(("col", "rep"), "row"),
        ),
        check_vma=False,
    )
```

profile of v0, /device:TPU:0, one launch (start us, length us, event | category | flops | bytes accessed | tf_op | source)
XLA Modules:
  0.0 577.4 jit_solution(1682216005050882857)
XLA Ops:
  7.2 0.7 all-gather.6.cloned.1.call-update
  7.9 0.7 all-gather.4.cloned.1.call-update
  8.7 73.5 %all-gather.6.cloned.1.call-done = bf16[1,2048,1664]{2,1,0:T(8,128)(2,1)} async-done(((bf16[1,512,1664]{2,1,0:T(8,128)(2,1)}), bf16[1,2048,1664]{2,1,0:T(8,128)(2,1)}) %all-gather.6.cloned.1.call-update) | async-done | bytes 6815760 | tf_op jit(solution)/shard_map/all_gather | solution.py:39
  82.2 76.4 %all-gather.4.cloned.1.call-done = bf16[1,2048,2048]{2,1,0:T(8,128)(2,1)} async-done(((bf16[1,128,2048]{2,1,0:T(8,128)(2,1)}), bf16[1,2048,2048]{2,1,0:T(8,128)(2,1)}) %all-gather.4.cloned.1.call-update) | async-done | bytes 8388624 | tf_op jit(solution)/shard_map/all_gather | solution.py:37
  158.6 21.5 %fusion = f32[2048,1664]{1,0:T(8,128)} fusion(bf16[1,2048,2048]{2,1,0:T(8,128)(2,1)} %all-gather.4.cloned.1.call-done, bf16[1,2048,1664]{2,1,0:T(8,128)(2,1)} %all-gather.6.cloned.1.call-done), kind=kOutput, calls=%fused_computation.1 | convolution fusion | flops 13958643712 | bytes 28835840 | tf_op jit(solution)/shard_map/dot_general | solution.py:22
  180.2 0.2 all-gather.8.cloned.1.call-start
  180.4 0.4 copy-done.2
  180.8 0.1 copy.44
  180.9 0.1 copy.46
  181.0 0.1 copy.48
  181.1 0.5 mul.75
  181.6 4.6 copy.77
  186.1 8.2 %copy.49 = f32[1024,1664]{1,0:T(8,128)} copy(f32[1024,1664]{0,1:T(8,128)} %bitcast.65) | data formatting | bytes 13631488 | tf_op jit(solution)/shard_map/mul | solution.py:10
  194.3 0.5 mul.69
  194.8 4.6 copy.78
  199.4 7.7 %copy.47 = f32[1024,1664]{1,0:T(8,128)} copy(f32[1024,1664]{0,1:T(8,128)} %bitcast.67) | data formatting | bytes 13631488 | tf_op jit(solution)/shard_map/mul | solution.py:10
  207.1 0.5 mul.66
  207.6 4.6 copy.79
  212.2 7.8 %copy.45 = f32[1024,1664]{1,0:T(8,128)} copy(f32[1024,1664]{0,1:T(8,128)} %bitcast.69) | data formatting | bytes 13631488 | tf_op jit(solution)/shard_map/mul | solution.py:10
  220.0 116.3 %reduce-scatter.2.cloned.1.call-done = f32[1024,1664]{1,0:T(8,128)} async-done(((f32[2048,1664]{1,0:T(8,128)}), f32[1024,1664]{1,0:T(8,128)}) %reduce-scatter.2.cloned.1.call-update) | async-done | bytes 6815760 | tf_op jit(solution)/shard_map/reduce_scatter | solution.py:41
  336.3 17.2 %fusion.7 = (f32[1024,1664]{1,0:T(8,128)}, f32[1024,1664]{1,0:T(8,128)}, f32[1024,1664]{1,0:T(8,128)}, f32[1024,1664]{1,0:T(8,128)}) fusion(f32[1024,1664]{1,0:T(8,128)} %reduce-scatter.2.cloned.1.call-done, f32[1024,1664]{1,0:T(8,128)} %copy.47, bf16[1024,1664]{1,0:T(8,128)(2,1)S(1)} %copy-done.1, f32[1024,1664]{1,0:T(8,128)} %copy.49, ...), kind=kLoop, calls=%fused_computation.21 | loop fusion | flops 22151168 | bytes 54525952 | tf_op jit(solution)/shard_map/abs | solution.py:16
  353.5 7.7 %copy.53 = f32[1024,1664]{0,1:T(8,128)} copy(f32[1024,1664]{1,0:T(8,128)} %get-tuple-element.20) | data formatting | bytes 13631488 | tf_op jit(solution)/shard_map/abs | solution.py:16
  361.2 7.5 %copy.64 = f32[208,8,8,128]{3,2,1,0:T(8,128)} copy(f32[208,8,8,128]{3,1,2,0:T(8,128)} %bitcast.70) | data formatting | bytes 13631488
  368.7 3.4 reduce_max.28
  372.1 0.5 div.56
  372.6 4.6 copy.75
  377.2 7.7 %copy.54 = f32[1024,1664]{1,0:T(8,128)} copy(f32[1024,1664]{0,1:T(8,128)} %bitcast.72) | data formatting | bytes 13631488 | tf_op jit(solution)/shard_map/div | solution.py:17
  384.8 7.6 %copy.55 = f32[1024,1664]{0,1:T(8,128)} copy(f32[1024,1664]{1,0:T(8,128)} %get-tuple-element.26) | data formatting | bytes 13631488 | tf_op jit(solution)/shard_map/abs | solution.py:16
  392.4 7.4 %copy.66 = f32[208,8,8,128]{3,2,1,0:T(8,128)} copy(f32[208,8,8,128]{3,1,2,0:T(8,128)} %bitcast.73) | data formatting | bytes 13631488
  399.9 3.4 reduce_max.29
  403.3 0.5 div.59
  403.8 4.6 copy.74
  408.3 7.8 %copy.56 = f32[1024,1664]{1,0:T(8,128)} copy(f32[1024,1664]{0,1:T(8,128)} %bitcast.75) | data formatting | bytes 13631488 | tf_op jit(solution)/shard_map/div | solution.py:17
  416.2 19.6 %fusion.8 = (f32[1024,1664]{1,0:T(8,128)}, f32[1024,1664]{1,0:T(8,128)}, bf16[1024,1664]{1,0:T(8,128)(2,1)}, bf16[1024,1664]{1,0:T(8,128)(2,1)}) fusion(f32[1024,1664]{1,0:T(8,128)} %get-tuple-element.27, f32[1024,1664]{1,0:T(8,128)} %get-tuple-element.21, f32[1024,1664]{1,0:T(8,128)} %copy.45, bf16[1024,1664]{1,0:T(8,128)(2,1)S(1)} %copy-done, ...), kind=kLoop, calls=%fused_computation.22 | loop fusion | flops 25559040 | bytes 57933824 | tf_op jit(solution)/shard_map/abs | solution.py:16
  435.8 7.6 %copy.50 = f32[1024,1664]{0,1:T(8,128)} copy(f32[1024,1664]{1,0:T(8,128)} %get-tuple-element.22) | data formatting | bytes 13631488 | tf_op jit(solution)/shard_map/abs | solution.py:16
  443.4 7.5 %copy.62 = f32[208,8,8,128]{3,2,1,0:T(8,128)} copy(f32[208,8,8,128]{3,1,2,0:T(8,128)} %bitcast.76) | data formatting | bytes 13631488
  450.9 3.4 reduce_max.27
  454.3 0.5 div.53
  454.9 4.6 copy.76
  459.4 7.7 %copy.51 = f32[1024,1664]{1,0:T(8,128)} copy(f32[1024,1664]{0,1:T(8,128)} %bitcast.78) | data formatting | bytes 13631488 | tf_op jit(solution)/shard_map/div | solution.py:17
  467.1 7.6 %divide_convert_fusion.2 = bf16[1024,1664]{1,0:T(8,128)(2,1)} fusion(f32[1024,1664]{1,0:T(8,128)} %get-tuple-element.23, f32[1024,1664]{1,0:T(8,128)} %copy.51), kind=kLoop, calls=%fused_computation.13 | loop fusion | flops 3407872 | bytes 17039360 | tf_op jit(solution)/shard_map/convert_element_type | solution.py:17
  474.7 0.7 copy.57
  475.3 0.7 copy.58
  476.0 0.1 copy.52
  476.1 4.3 all_gather.15
  480.4 0.6 convert_element_type.29
  481.0 83.6 %all-gather.8.cloned.1.call-done = bf16[2048,1664]{1,0:T(8,128)(2,1)} async-done(((bf16[1024,1664]{1,0:T(8,128)(2,1)}), bf16[2048,1664]{1,0:T(8,128)(2,1)}) %all-gather.8.cloned.1.call-update) | async-done | bytes 6815760 | tf_op jit(solution)/shard_map/all_gather | solution.py:55
  564.6 6.3 %copy.81 = bf16[2048,1664]{1,0:T(8,128)(2,1)} copy(bf16[2048,1664]{1,0:T(8,128)(2,1)} %all-gather.8.cloned.1.call-done) | data formatting | bytes 13631488
  (17 shorter events, 0.2 us)
Async XLA Ops:
  7.2 75.0 %all-gather.6.cloned.1.call-start = ((), (), s32[]{:S(2)}) async-start(), calls=%async_computation.2 | async-start | bytes 8519680 | tf_op jit(solution)/shard_map/all_gather | solution.py:39
  7.9 150.7 %all-gather.4.cloned.1.call-start = ((), (), s32[]{:S(2)}) async-start(), calls=%async_computation.1 | async-start | bytes 8912896 | tf_op jit(solution)/shard_map/all_gather | solution.py:37
  8.6 327.7 %reduce-scatter.2.cloned.1.call-start = ((), (), s32[]{:S(2)}) async-start(), calls=%async_computation.3 | async-start | bytes 20447232 | tf_op jit(solution)/shard_map/reduce_scatter | solution.py:41
  180.1 0.7 copy-start.2
  180.1 0.8 copy-start.3
  180.1 0.9 copy-start.4
  180.2 384.4 %all-gather.8.cloned.1.call-start = ((), (), s32[]{:S(2)}) async-start(), calls=%async_computation.4 | async-start | bytes 10223616 | tf_op jit(solution)/shard_map/all_gather | solution.py:55
  212.2 124.1 %copy-start.1 = (bf16[1024,1664]{1,0:T(8,128)(2,1)S(1)}, bf16[1024,1664]{1,0:T(8,128)(2,1)}, u32[]{:S(2)}) copy-start(bf16[1024,1664]{1,0:T(8,128)(2,1)} %param.12) | copy-start | bytes 10223620
  408.3 7.8 %copy-start = (bf16[1024,1664]{1,0:T(8,128)(2,1)S(1)}, bf16[1024,1664]{1,0:T(8,128)(2,1)}, u32[]{:S(2)}) copy-start(bf16[1024,1664]{1,0:T(8,128)(2,1)} %param.10) | copy-start | bytes 10223620
Sparse Core Ops, SparseCore 0:
  9.7 72.4 all-gather.5
  84.7 73.8 all-gather.3
  180.3 155.9 reduce-scatter.1
  474.8 89.7 all-gather.7
where the time goes:
time: 579 us; the launch traced here: 577 us
  waiting for transfers between devices  351 us (61%)
  local copies, waits for them, and re-layouts  131 us (23%)
  other arithmetic  55.3 us (10%)
  matrix products  21.5 us (4%)
  between operations  13.8 us (2%)
    reduce_scatter x1, waiting for transfers between devices, per_device(): lax.psum_scatter(partial_value, 'rep', scatter_dimension=0, tiled=True)  116 us
    all_gather x1, waiting for transfers between devices, per_device(): lax.all_gather(codes_w, 'rep', axis=0, tiled=True)  83.6 us
    all_gather x1, waiting for transfers between devices, per_device(): gathered = lax.all_gather(activations, 'row', axis=1, tiled=True)[0]  76.4 us
    all_gather x1, waiting for transfers between devices, per_device(): lax.all_gather(out_grads, 'col', axis=1, tiled=True)[0]  73.5 us
    unnamed x25, local copies, waits for them, and re-layouts  58 us
    abs x2, other arithmetic, quantize(): scales = jnp.max(jnp.abs(blocks), axis=(1, 3)) + 1e-06  36.9 us
    mul x6, local copies, waits for them, and re-layouts, dequantize(): return (blocks * scales[:, None, :, None]).reshape(rows, cols)  25.3 us
    div x6, local copies, waits for them, and re-layouts, quantize(): blocks / scales[:, None, :, None]  24.7 us
  transfers between devices with their start and end apart: 4, of which 4 were waited for; matrix products, arithmetic and copies ran while one was open for 7% of the time, Pallas kernels for 0%

commit v1 on v0

v1 whole, which is shorter than its diff:
```python
import jax
import jax.numpy as jnp
from jax import lax
from jax.experimental import pallas as pl
from jax.experimental.pallas import tpu as pltpu
from jax.sharding import PartitionSpec as P

MESH = pl.DeviceIdType.MESH
F32 = jnp.float32
BF16 = jnp.bfloat16
CHUNKS = 13
BIAS_ONE = 1.0 - 0.9**10
BIAS_TWO = 1.0 - 0.95**10


def kernel(
    acts, grads, w_scale, m_scale, v_scale, w_code, m_code, v_code,
    w_out, ws_out, m_out, ms_out, v_out, vs_out,
    A, T, G, W, M, V, acc, new, peak, inv, scales, peer_scales,
    in_sem, own_sem, y_send, y_recv, z_send, z_recv, zf_send, zf_recv, sib_send, sib_recv,
    s1_send, s1_recv, sx_send, sx_recv, s4_send, s4_recv,
    w_send, w_recv, sc_send, sc_recv, wl_sem, m_sem, v_sem,
):
    r, c, p = lax.axis_index("row"), lax.axis_index("col"), lax.axis_index("rep")
    yh, z, k = r // 8, (r // 2) % 4, r % 2
    q, yo = 1 - p, 1 - yh

    def at(yh_, z_, k_, c_, p_):
        return (yh_ * 8 + z_ * 2 + k_, c_, p_)

    partner = at(yh, z, k, c, q)
    other = at(yo, z, k, c, q)
    across = at(yo, z, k, c, p)
    sibling = at(yh, z, 1 - k, c, p)
    z_next, z_prev, z_far = (z + 1) % 4, (z + 3) % 4, (z + 2) % 4
    c_next, c_prev, c_far = (c + 1) % 4, (c + 3) % 4, (c + 2) % 4
    z_dev = (at(yh, z_next, k, c, p), at(yh, z_prev, k, c, p))
    x_dev = (at(yh, z, k, c_next, p), at(yh, z, k, c_prev, p))

    def remote(src, dst, send, recv, device):
        return pltpu.make_async_remote_copy(
            src_ref=src, dst_ref=dst, send_sem=send, recv_sem=recv,
            device_id=device, device_id_type=MESH,
        )

    def own_rows(part, c_):
        return pl.ds(pl.multiple_of(c_ * 1024 + part * 512, 512), 512)

    def cols(j):
        return pl.ds(pl.multiple_of(j * 128, 128), 128)

    def load_own(j):
        return pltpu.make_async_copy(grads.at[:, cols(j)], G.at[j, own_rows(p, c)], own_sem.at[j])

    def start_own(j, carry):
        load_own(j).start()
        return carry

    lax.fori_loop(0, CHUNKS, start_own, 0)
    loads = [
        pltpu.make_async_copy(w_code, W, in_sem.at[0]),
        pltpu.make_async_copy(m_code, M, in_sem.at[1]),
        pltpu.make_async_copy(v_code, V, in_sem.at[2]),
    ]
    for load in loads:
        load.start()

    barrier = pltpu.get_barrier_semaphore()
    for device in (partner, other, across, sibling) + z_dev + x_dev:
        pl.semaphore_signal(barrier, inc=1, device_id=device, device_id_type=MESH)

    def idx(yh_, z_, k_, p_):
        return (yh_ * 2 + z_ // 2) * 8 + p_ * 4 + (z_ % 2) * 2 + k_

    mine = idx(yh, z, k, p)
    for i in range(8):
        A[mine, i * 128:(i + 1) * 128, :] = acts[:, pl.ds(pl.multiple_of(p * 1024 + i * 128, 128), 128)].T
        T[i * 128:(i + 1) * 128, :] = acts[:, pl.ds(pl.multiple_of(q * 1024 + i * 128, 128), 128)].T

    pl.semaphore_wait(barrier, 8)

    piece_yh = (yh, yh, yo, yo)
    piece_p = (p, q, q, p)

    def piece(i, z_, k_):
        return A.at[idx(piece_yh[i], z_, k_, piece_p[i])]

    def y_copy(i):
        src = A.at[mine] if i == 3 else T
        return remote(src, A.at[mine], y_send.at[i], y_recv.at[i], (None, partner, other, across)[i])

    def y_landed(i):
        got = piece(i, z, k)
        return remote(got, got, y_send.at[i], y_recv.at[i], (None, partner, other, across)[i])

    def z_copy(i, d):
        return remote(piece(i, z, k), piece(i, z, k), z_send.at[d, i], z_recv.at[d, i], z_dev[d])

    def z_landed(i, d):
        got = piece(i, (z_prev, z_next)[d], k)
        return remote(got, got, z_send.at[d, i], z_recv.at[d, i], z_dev[d])

    def zf_copy(i):
        d = i // 2
        got = piece(i, (z_prev, z_next)[d], k)
        return remote(got, got, zf_send.at[i], zf_recv.at[i], z_dev[d])

    def zf_landed(i):
        got = piece(i, z_far, k)
        return remote(got, got, zf_send.at[i], zf_recv.at[i], z_dev[i // 2])

    hops = (z, z_prev, z_next, z_far)

    def sib_copy(i, h):
        got = piece(i, hops[h], k)
        return remote(got, got, sib_send.at[h, i], sib_recv.at[h, i], sibling)

    def sib_landed(i, h):
        got = piece(i, hops[h], 1 - k)
        return remote(got, got, sib_send.at[h, i], sib_recv.at[h, i], sibling)

    def s1_copy(j):
        rows = G.at[j, own_rows(p, c)]
        return remote(rows, rows, s1_send.at[j], s1_recv.at[j], partner)

    def s1_landed(j):
        rows = G.at[j, own_rows(q, c)]
        return remote(rows, rows, s1_send.at[j], s1_recv.at[j], partner)

    def sx_copy(j, part, d):
        rows = G.at[j, own_rows((p, q)[part], c)]
        return remote(rows, rows, sx_send.at[part, d, j], sx_recv.at[part, d, j], x_dev[d])

    def sx_landed(j, part, d):
        rows = G.at[j, own_rows((p, q)[part], (c_prev, c_next)[d])]
        return remote(rows, rows, sx_send.at[part, d, j], sx_recv.at[part, d, j], x_dev[d])

    def s4_copy(j, d):
        rows = G.at[j, own_rows((p, q)[d], (c_prev, c_next)[d])]
        return remote(rows, rows, s4_send.at[d, j], s4_recv.at[d, j], x_dev[d])

    def s4_landed(j, d):
        rows = G.at[j, own_rows((p, q)[d], c_far)]
        return remote(rows, rows, s4_send.at[d, j], s4_recv.at[d, j], x_dev[d])

    def send_own(j):
        sx_copy(j, 0, 0).start()
        sx_copy(j, 0, 1).start()

    def send_partner(j):
        s1_landed(j).wait_recv()
        sx_copy(j, 1, 0).start()
        sx_copy(j, 1, 1).start()

    def forward(j):
        sx_landed(j, 0, 0).wait_recv()
        s4_copy(j, 0).start()
        sx_landed(j, 1, 1).wait_recv()
        s4_copy(j, 1).start()

    def x_step(j):
        forward(j)

        @pl.when(j + 2 < CHUNKS)
        def _():
            send_own(j + 2)
            send_partner(j + 2)

    for i in (1, 2, 3):
        y_copy(i).start()
    z_copy(0, 0).start()
    z_copy(0, 1).start()
    sib_copy(0, 0).start()

    def wait_own(j, carry):
        load_own(j).wait()
        return carry

    lax.fori_loop(0, CHUNKS, wait_own, 0)

    def start_s1(j, carry):
        s1_copy(j).start()
        return carry

    lax.fori_loop(0, CHUNKS, start_s1, 0)
    send_own(0)
    send_own(1)

    for i in (1, 2, 3):
        y_landed(i).wait_recv()
        z_copy(i, 0).start()
        z_copy(i, 1).start()
        sib_copy(i, 0).start()
    send_partner(0)
    send_partner(1)

    for i in range(4):
        z_landed(i, 0).wait_recv()
        if i < 2:
            zf_copy(i).start()
        sib_copy(i, 1).start()
        z_landed(i, 1).wait_recv()
        if i >= 2:
            zf_copy(i).start()
        sib_copy(i, 2).start()
        x_step(i)
    for i in range(4):
        zf_landed(i).wait_recv()
        sib_copy(i, 3).start()
    x_step(4)
    for load in loads:
        load.wait()
    for h in range(4):
        for i in range(4):
            sib_landed(i, h).wait_recv()

    lane = lax.broadcasted_iota(jnp.int32, (24, 128), 1)

    def w_copy(j):
        here = pl.ds(pl.multiple_of(p * 1024, 1024), 1024)
        return remote(W.at[:, cols(j)], w_out.at[here, cols(j)], w_send.at[j], w_recv.at[j], partner)

    def w_landed(j):
        there = pl.ds(pl.multiple_of(q * 1024, 1024), 1024)
        return remote(W.at[:, cols(j)], w_out.at[there, cols(j)], w_send.at[j], w_recv.at[j], partner)

    def stores(j):
        here = pl.ds(pl.multiple_of(p * 1024, 1024), 1024)
        return (
            pltpu.make_async_copy(W.at[:, cols(j)], w_out.at[here, cols(j)], wl_sem.at[j]),
            pltpu.make_async_copy(M.at[:, cols(j)], m_out.at[:, cols(j)], m_sem.at[j]),
            pltpu.make_async_copy(V.at[:, cols(j)], v_out.at[:, cols(j)], v_sem.at[j]),
        )

    def chunk(j, carry):
        step = 4 + (2 * j) // 3

        @pl.when(jnp.logical_and(j > 0, step != 4 + (2 * (j - 1)) // 3))
        def _():
            x_step(step)

        sx_landed(j, 1, 0).wait_recv()
        sx_landed(j, 0, 1).wait_recv()
        s4_landed(j, 0).wait_recv()
        s4_landed(j, 1).wait_recv()
        left = jnp.concatenate([A[i] for i in range(32)], axis=1)
        acc[...] = jnp.dot(left, G[j], preferred_element_type=F32)

        def update(d, carry):
            rows = pl.ds(pl.multiple_of(d * 128, 128), 128)
            g = acc[rows, :]
            weight = W[rows, cols(j)].astype(F32) * w_scale[d, j]
            moment = M[rows, cols(j)].astype(F32) * m_scale[d, j]
            second = V[rows, cols(j)].astype(F32) * v_scale[d, j]
            moment1 = 0.9 * moment + 0.1 * g
            second1 = 0.95 * second + 0.05 * (g * g)
            u = second1 * (1.0 / BIAS_TWO)
            denom = u * lax.rsqrt(u) + 1e-08
            weight1 = weight - 0.01 * ((moment1 * (1.0 / BIAS_ONE)) / denom + 0.1 * weight)
            for n, value in enumerate((weight1, moment1, second1)):
                new[n, rows, :] = value
                peak[n * 8 + d] = jnp.max(jnp.abs(value).reshape(16, 8, 128), axis=0)
            return carry

        lax.fori_loop(0, 8, update, 0)
        scale = jnp.max(jnp.max(peak[...], axis=1), axis=1, keepdims=True) + 1e-06
        scale = jnp.broadcast_to(scale, (24, 128))
        scales[...] = jnp.where(lane == j, scale, scales[...])
        inv[...] = 1.0 / scale

        def encode(d, carry):
            rows = pl.ds(pl.multiple_of(d * 128, 128), 128)
            for n, out in enumerate((W, M, V)):
                out[rows, cols(j)] = (new[n, rows, :] * inv[pl.ds(n * 8 + d, 1), :]).astype(BF16)
            return carry

        lax.fori_loop(0, 8, encode, 0)
        w_copy(j).start()
        for store in stores(j):
            store.start()
        return carry

    scales[...] = jnp.zeros_like(scales)
    lax.fori_loop(0, CHUNKS, chunk, 0)

    sc_copy = remote(scales.at[0:8], peer_scales, sc_send.at[0], sc_recv.at[0], partner)
    sc_copy.start()
    ms_out[...] = scales[8:16, :CHUNKS]
    vs_out[...] = scales[16:24, :CHUNKS]
    ws_out[pl.ds(pl.multiple_of(p * 8, 8), 8), :] = scales[0:8, :CHUNKS]

    for i in (1, 2, 3):
        y_copy(i).wait_send()
    for i in range(4):
        z_copy(i, 0).wait_send()
        z_copy(i, 1).wait_send()
        zf_copy(i).wait_send()
        for h in range(4):
            sib_copy(i, h).wait_send()

    def drain(j, carry):
        s1_copy(j).wait_send()
        for d in range(2):
            sx_copy(j, 0, d).wait_send()
            sx_copy(j, 1, d).wait_send()
            s4_copy(j, d).wait_send()
        for store in stores(j):
            store.wait()
        w_copy(j).wait_send()
        w_landed(j).wait_recv()
        return carry

    lax.fori_loop(0, CHUNKS, drain, 0)
    sc_copy.wait()
    ws_out[pl.ds(pl.multiple_of(q * 8, 8), 8), :] = peer_scales[:, :CHUNKS]


def per_device(
    activations, out_grads, weight_code, weight_scale,
    moment_code, moment_scale, second_code, second_scale,
):
    vmem = pl.BlockSpec(memory_space=pltpu.VMEM)
    smem = pl.BlockSpec(memory_space=pltpu.SMEM)
    hbm = pl.BlockSpec(memory_space=pl.ANY)
    dma = pltpu.SemaphoreType.DMA
    shape = jax.ShapeDtypeStruct
    return pl.pallas_call(
        kernel,
        out_shape=(
            shape((2048, 1664), BF16), shape((16, 13), F32),
            shape((1024, 1664), BF16), shape((8, 13), F32),
            shape((1024, 1664), BF16), shape((8, 13), F32),
        ),
        in_specs=[vmem, hbm, smem, smem, smem, hbm, hbm, hbm],
        out_specs=(hbm, vmem, hbm, vmem, hbm, vmem),
        scratch_shapes=[
            pltpu.VMEM((32, 1024, 128), BF16),
            pltpu.VMEM((1024, 128), BF16),
            pltpu.VMEM((CHUNKS, 4096, 128), BF16),
            pltpu.VMEM((1024, 1664), BF16),
            pltpu.VMEM((1024, 1664), BF16),
            pltpu.VMEM((1024, 1664), BF16),
            pltpu.VMEM((1024, 128), F32),
            pltpu.VMEM((3, 1024, 128), F32),
            pltpu.VMEM((24, 8, 128), F32),
            pltpu.VMEM((24, 128), F32),
            pltpu.VMEM((24, 128), F32),
            pltpu.VMEM((8, 128), F32),
            dma((3,)), dma((CHUNKS,)),
            dma((4,)), dma((4,)),
            dma((2, 4)), dma((2, 4)),
            dma((4,)), dma((4,)),
            dma((4, 4)), dma((4, 4)),
            dma((CHUNKS,)), dma((CHUNKS,)),
            dma((2, 2, CHUNKS)), dma((2, 2, CHUNKS)),
            dma((2, CHUNKS)), dma((2, CHUNKS)),
            dma((CHUNKS,)), dma((CHUNKS,)),
            dma((1,)), dma((1,)),
            dma((CHUNKS,)), dma((CHUNKS,)), dma((CHUNKS,)),
        ],
        compiler_params=pltpu.CompilerParams(
            collective_id=0, has_side_effects=True, vmem_limit_bytes=56 << 20
        ),
        cost_estimate=pl.CostEstimate(
            flops=2 * 1024 * 1664 * 4096, bytes_accessed=26 << 20, transcendentals=2 * 1024 * 1664
        ),
    )(
        activations[0], out_grads[0], weight_scale, moment_scale, second_scale,
        weight_code, moment_code, second_code,
    )


def solution(mesh):
    return jax.shard_map(
        per_device,
        mesh=mesh,
        in_specs=(
            P("rep", "row", "col"),
            P("rep", "col", "row"),
            P(("col", "rep"), "row"),
            P(("col", "rep"), "row"),
            P(("col", "rep"), "row"),
            P(("col", "rep"), "row"),
            P(("col", "rep"), "row"),
            P(("col", "rep"), "row"),
        ),
        out_specs=(
            P("col", "row"),
            P("col", "row"),
            P(("col", "rep"), "row"),
            P(("col", "rep"), "row"),
            P(("col", "rep"), "row"),
            P(("col", "rep"), "row"),
        ),
        check_vma=False,
    )
```

time: 579 us -> 160 us (0.28)
  waiting for transfers between devices: 351 us -> 0 us
  Pallas kernels: 0 us -> 147 us
  local copies, waits for them, and re-layouts: 131 us -> 12.6 us
  other arithmetic: 55.3 us -> 0 us
  matrix products: 21.5 us -> 0 us
  between operations: 13.8 us -> 0.67 us
    all_gather x3 -> x0, waiting for transfers between devices: 233 us -> none  [the longest x1 83.6 us: per_device(): lax.all_gather(codes_w, 'rep', axis=0, tiled=True)]
    pallas_call x0 -> x1, Pallas kernels: none -> 147 us  [per_device(): pl.pallas_call(kernel, out_shape=(shape((2048, 1664), BF16), shape((16, 1...]
    reduce_scatter x1 -> x0, waiting for transfers between devices: 116 us -> none  [per_device(): lax.psum_scatter(partial_value, 'rep', scatter_dimension=0, tiled=True)]
    unnamed x25 -> x16, local copies, waits for them, and re-layouts: 58 us -> 12.6 us
    abs x2 -> x0, other arithmetic: 36.9 us -> none  [quantize(): scales = jnp.max(jnp.abs(blocks), axis=(1, 3)) + 1e-06]
    mul x6 -> x0, local copies, waits for them, and re-layouts: 25.3 us -> none  [dequantize(): return (blocks * scales[:, None, :, None]).reshape(rows, cols)]
    div x6 -> x0, local copies, waits for them, and re-layouts: 24.7 us -> none  [quantize(): blocks / scales[:, None, :, None]]
    abs x3 -> x0, local copies, waits for them, and re-layouts: 22.9 us -> none  [quantize(): scales = jnp.max(jnp.abs(blocks), axis=(1, 3)) + 1e-06]
  transfers between devices with their start and end apart: 4 -> 0, of which waited for: 4 -> 0; matrix products, arithmetic and copies ran while one was open for 7% -> 0% of each run, Pallas kernels for 0% -> 0%
where the time goes in v1:
time: 160 us
  Pallas kernels  147 us (92%)
  local copies, waits for them, and re-layouts  12.6 us (8%)
    pallas_call x1, Pallas kernels, per_device(): pl.pallas_call(kernel, out_shape=(shape((2048, 1664), BF16), shape((16, 1...  147 us
    unnamed x16, local copies, waits for them, and re-layouts  12.6 us

profile of v1, /device:TPU:0, one launch (start us, length us, event | category | flops | bytes accessed | tf_op | source)
XLA Modules:
  0.0 160.2 jit_solution(6038851946287610261)
XLA Ops:
  0.6 146.9 %shard_map.127 = (bf16[2048,1664]{1,0:T(8,128)(2,1)}, f32[16,13]{1,0:T(8,128)}, bf16[1024,1664]{1,0:T(8,128)(2,1)}, f32[8,13]{1,0:T(8,128)}, bf16[1024,1664]{1,0:T(8,128)(2,1)}, /*index=5*/f32[8,13]{1,0:T(8,128)}) custom-call(bf16[128,2048]{1,0:T(8,128)(2,1)} %bitcast.3, bf16[512,1664]{1,0:T(8,128)(2,1)} %bitcast.2, f32[8,13]{1,0:T(8,128)} %w_scale.1, ...), custom_call_target="tpu_custom_call" | custom-call | flops 13958643712 | bytes 27262976 | tf_op jit(solution)/shard_map/pallas_call | solution.py:327
  147.5 0.0 copy-start.2
  147.5 0.0 copy-start.1
  147.6 6.5 %copy.20 = bf16[2048,1664]{1,0:T(8,128)(2,1)} copy(bf16[2048,1664]{1,0:T(8,128)(2,1)} %get-tuple-element.12) | data formatting | bytes 13631488
  154.0 0.0 copy-done.2
  154.0 0.6 copy.21
  154.6 0.0 copy-done.1
  154.6 0.0 copy-start.4
  154.6 0.0 copy-start
  154.6 1.8 %copy.22 = bf16[1024,1664]{1,0:T(8,128)(2,1)} copy(bf16[1024,1664]{1,0:T(8,128)(2,1)S(1)} %copy-done.1) | data formatting | bytes 6815744
  156.4 0.0 copy-done.4
  156.4 0.6 copy.23
  157.0 0.9 copy-done
  157.8 0.0 copy-start.3
  157.8 1.7 %copy.24 = bf16[1024,1664]{1,0:T(8,128)(2,1)} copy(bf16[1024,1664]{1,0:T(8,128)(2,1)S(1)} %copy-done) | data formatting | bytes 6815744
  159.6 0.0 copy-done.3
  159.6 0.6 copy.25
Async XLA Ops:
  147.5 6.5 %copy-start.2 = (f32[16,13]{1,0:T(8,128)S(1)}, f32[16,13]{1,0:T(8,128)}, u32[]{:S(2)}) copy-start(f32[16,13]{1,0:T(8,128)} %get-tuple-element.13) | copy-start | bytes 2500
  147.5 7.1 %copy-start.1 = (bf16[1024,1664]{1,0:T(8,128)(2,1)S(1)}, bf16[1024,1664]{1,0:T(8,128)(2,1)}, u32[]{:S(2)}) copy-start(bf16[1024,1664]{1,0:T(8,128)(2,1)} %get-tuple-element.14) | copy-start | bytes 10223620
  154.6 1.8 %copy-start.4 = (f32[8,13]{1,0:T(8,128)S(1)}, f32[8,13]{1,0:T(8,128)}, u32[]{:S(2)}) copy-start(f32[8,13]{1,0:T(8,128)} %get-tuple-element.15) | copy-start | bytes 1252
  154.6 3.2 %copy-start = (bf16[1024,1664]{1,0:T(8,128)(2,1)S(1)}, bf16[1024,1664]{1,0:T(8,128)(2,1)}, u32[]{:S(2)}) copy-start(bf16[1024,1664]{1,0:T(8,128)(2,1)} %get-tuple-element.16) | copy-start | bytes 10223620
  157.8 1.8 %copy-start.3 = (f32[8,13]{1,0:T(8,128)S(1)}, f32[8,13]{1,0:T(8,128)}, u32[]{:S(2)}) copy-start(f32[8,13]{1,0:T(8,128)} %get-tuple-element.17) | copy-start | bytes 1252

commit v2 on v1

--- a/solution.py
+++ b/solution.py
@@ -1,3 +1,5 @@
+import functools
+
 import jax
 import jax.numpy as jnp
 from jax import lax
@@ -14,12 +16,12 @@
 
 
 def kernel(
-    acts, grads, w_scale, m_scale, v_scale, w_code, m_code, v_code,
-    w_out, ws_out, m_out, ms_out, v_out, vs_out,
-    A, T, G, W, M, V, acc, new, peak, inv, scales, peer_scales,
+    acts_in, grads, w_scale, m_scale, v_scale, w_code, m_code, v_code,
+    W, peer_w, M, V, scales,
+    acts, A, T, G, acc, new, peak, inv,
     in_sem, own_sem, y_send, y_recv, z_send, z_recv, zf_send, zf_recv, sib_send, sib_recv,
     s1_send, s1_recv, sx_send, sx_recv, s4_send, s4_recv,
-    w_send, w_recv, sc_send, sc_recv, wl_sem, m_sem, v_sem,
+    w_send, w_recv, sc_send, sc_recv,
 ):
     r, c, p = lax.axis_index("row"), lax.axis_index("col"), lax.axis_index("rep")
     yh, z, k = r // 8, (r // 2) % 4, r % 2
@@ -62,12 +64,15 @@
         pltpu.make_async_copy(m_code, M, in_sem.at[1]),
         pltpu.make_async_copy(v_code, V, in_sem.at[2]),
     ]
-    for load in loads:
-        load.start()
+    load_acts = pltpu.make_async_copy(acts_in, acts, in_sem.at[3])
+    load_acts.start()
 
     barrier = pltpu.get_barrier_semaphore()
     for device in (partner, other, across, sibling) + z_dev + x_dev:
         pl.semaphore_signal(barrier, inc=1, device_id=device, device_id_type=MESH)
+
+    scales[0:24, :] = jnp.zeros((24, 128), F32)
+    load_acts.wait()
 
     def idx(yh_, z_, k_, p_):
         return (yh_ * 2 + z_ // 2) * 8 + p_ * 4 + (z_ % 2) * 2 + k_
@@ -161,40 +166,16 @@
     def x_step(j):
         forward(j)
 
-        @pl.when(j + 2 < CHUNKS)
+        @pl.when(j < 3)
         def _():
+            send_partner(j + 3)
+
+        @pl.when(jnp.logical_and(j > 3, j < CHUNKS - 2))
+        def _():
+            send_partner(j + 2)
             send_own(j + 2)
-            send_partner(j + 2)
-
-    for i in (1, 2, 3):
-        y_copy(i).start()
-    z_copy(0, 0).start()
-    z_copy(0, 1).start()
-    sib_copy(0, 0).start()
-
-    def wait_own(j, carry):
-        load_own(j).wait()
-        return carry
-
-    lax.fori_loop(0, CHUNKS, wait_own, 0)
-
-    def start_s1(j, carry):
-        s1_copy(j).start()
-        return carry
-
-    lax.fori_loop(0, CHUNKS, start_s1, 0)
-    send_own(0)
-    send_own(1)
-
-    for i in (1, 2, 3):
-        y_landed(i).wait_recv()
-        z_copy(i, 0).start()
-        z_copy(i, 1).start()
-        sib_copy(i, 0).start()
-    send_partner(0)
-    send_partner(1)
-
-    for i in range(4):
+
+    def relay(i):
         z_landed(i, 0).wait_recv()
         if i < 2:
             zf_copy(i).start()
@@ -203,10 +184,61 @@
         if i >= 2:
             zf_copy(i).start()
         sib_copy(i, 2).start()
-        x_step(i)
-    for i in range(4):
+
+    def spread(i):
+        y_landed(i).wait_recv()
+        z_copy(i, 0).start()
+        z_copy(i, 1).start()
+        sib_copy(i, 0).start()
+
+    def finish(i):
         zf_landed(i).wait_recv()
         sib_copy(i, 3).start()
+
+    for i in (1, 2, 3):
+        y_copy(i).start()
+    z_copy(0, 0).start()
+    z_copy(0, 1).start()
+
+    def wait_own(j, carry):
+        load_own(j).wait()
+        return carry
+
+    lax.fori_loop(0, CHUNKS, wait_own, 0)
+
+    def start_own_sends(j, carry):
+        send_own(j)
+        return carry
+
+    lax.fori_loop(0, 6, start_own_sends, 0)
+
+    def start_s1(j, carry):
+        s1_copy(j).start()
+        return carry
+
+    lax.fori_loop(0, CHUNKS, start_s1, 0)
+    sib_copy(0, 0).start()
+    for load in loads:
+        load.start()
+
+    spread(1)
+    spread(2)
+    relay(0)
+    spread(3)
+    relay(1)
+    send_partner(0)
+    send_partner(1)
+    relay(2)
+    send_partner(2)
+    x_step(0)
+    x_step(1)
+    x_step(2)
+    relay(3)
+    finish(0)
+    finish(2)
+    x_step(3)
+    finish(1)
+    finish(3)
     x_step(4)
     for load in loads:
         load.wait()
@@ -217,27 +249,16 @@
     lane = lax.broadcasted_iota(jnp.int32, (24, 128), 1)
 
     def w_copy(j):
-        here = pl.ds(pl.multiple_of(p * 1024, 1024), 1024)
-        return remote(W.at[:, cols(j)], w_out.at[here, cols(j)], w_send.at[j], w_recv.at[j], partner)
-
-    def w_landed(j):
-        there = pl.ds(pl.multiple_of(q * 1024, 1024), 1024)
-        return remote(W.at[:, cols(j)], w_out.at[there, cols(j)], w_send.at[j], w_recv.at[j], partner)
-
-    def stores(j):
-        here = pl.ds(pl.multiple_of(p * 1024, 1024), 1024)
-        return (
-            pltpu.make_async_copy(W.at[:, cols(j)], w_out.at[here, cols(j)], wl_sem.at[j]),
-            pltpu.make_async_copy(M.at[:, cols(j)], m_out.at[:, cols(j)], m_sem.at[j]),
-            pltpu.make_async_copy(V.at[:, cols(j)], v_out.at[:, cols(j)], v_sem.at[j]),
-        )
+        return remote(W.at[:, cols(j)], peer_w.at[:, cols(j)], w_send.at[j], w_recv.at[j], partner)
 
     def chunk(j, carry):
-        step = 4 + (2 * j) // 3
-
-        @pl.when(jnp.logical_and(j > 0, step != 4 + (2 * (j - 1)) // 3))
+        @pl.when(j == 3)
         def _():
-            x_step(step)
+            x_step(5)
+
+        @pl.when(jnp.logical_and(j > 4, j < CHUNKS - 1))
+        def _():
+            x_step(j + 1)
 
         sx_landed(j, 1, 0).wait_recv()
         sx_landed(j, 0, 1).wait_recv()
@@ -265,7 +286,7 @@
         lax.fori_loop(0, 8, update, 0)
         scale = jnp.max(jnp.max(peak[...], axis=1), axis=1, keepdims=True) + 1e-06
         scale = jnp.broadcast_to(scale, (24, 128))
-        scales[...] = jnp.where(lane == j, scale, scales[...])
+        scales[0:24, :] = jnp.where(lane == j, scale, scales[0:24, :])
         inv[...] = 1.0 / scale
 
         def encode(d, carry):
@@ -276,18 +297,12 @@
 
         lax.fori_loop(0, 8, encode, 0)
         w_copy(j).start()
-        for store in stores(j):
-            store.start()
-        return carry
-
-    scales[...] = jnp.zeros_like(scales)
+        return carry
+
     lax.fori_loop(0, CHUNKS, chunk, 0)
 
-    sc_copy = remote(scales.at[0:8], peer_scales, sc_send.at[0], sc_recv.at[0], partner)
+    sc_copy = remote(scales.at[0:8], scales.at[24:32], sc_send.at[0], sc_recv.at[0], partner)
     sc_copy.start()
-    ms_out[...] = scales[8:16, :CHUNKS]
-    vs_out[...] = scales[16:24, :CHUNKS]
-    ws_out[pl.ds(pl.multiple_of(p * 8, 8), 8), :] = scales[0:8, :CHUNKS]
 
     for i in (1, 2, 3):
         y_copy(i).wait_send()
@@ -304,15 +319,35 @@
             sx_copy(j, 0, d).wait_send()
             sx_copy(j, 1, d).wait_send()
             s4_copy(j, d).wait_send()
-        for store in stores(j):
-            store.wait()
-        w_copy(j).wait_send()
-        w_landed(j).wait_recv()
+        w_copy(j).wait()
         return carry
 
     lax.fori_loop(0, CHUNKS, drain, 0)
     sc_copy.wait()
-    ws_out[pl.ds(pl.multiple_of(q * 8, 8), 8), :] = peer_scales[:, :CHUNKS]
+
+
+def store_kernel(W, peer_w, M, V, scales, w_out, ws_out, m_out, ms_out, v_out, vs_out, sem):
+    p = lax.axis_index("rep")
+    q = 1 - p
+    copies = []
+    for n in range(4):
+        rows = pl.ds(n * 256, 256)
+        here = pl.ds(pl.multiple_of(p * 1024 + n * 256, 256), 256)
+        there = pl.ds(pl.multiple_of(q * 1024 + n * 256, 256), 256)
+        copies += [
+            pltpu.make_async_copy(W.at[rows], w_out.at[here], sem.at[0, n]),
+            pltpu.make_async_copy(peer_w.at[rows], w_out.at[there], sem.at[1, n]),
+            pltpu.make_async_copy(M.at[rows], m_out.at[rows], sem.at[2, n]),
+            pltpu.make_async_copy(V.at[rows], v_out.at[rows], sem.at[3, n]),
+        ]
+    for copy in copies:
+        copy.start()
+    ws_out[pl.ds(pl.multiple_of(p * 8, 8), 8), :] = scales[0:8, :CHUNKS]
+    ws_out[pl.ds(pl.multiple_of(q * 8, 8), 8), :] = scales[24:32, :CHUNKS]
+    ms_out[...] = scales[8:16, :CHUNKS]
+    vs_out[...] = scales[16:24, :CHUNKS]
+    for copy in copies:
+        copy.wait()
 
 
 def per_device(
@@ -324,29 +359,23 @@
     hbm = pl.BlockSpec(memory_space=pl.ANY)
     dma = pltpu.SemaphoreType.DMA
     shape = jax.ShapeDtypeStruct
-    return pl.pallas_call(
+    pinned = functools.partial(pltpu.with_memory_space_constraint, memory_space=pltpu.HBM)
+    codes = pltpu.VMEM((1024, 1664), BF16)
+    held = pl.pallas_call(
         kernel,
-        out_shape=(
-            shape((2048, 1664), BF16), shape((16, 13), F32),
-            shape((1024, 1664), BF16), shape((8, 13), F32),
-            shape((1024, 1664), BF16), shape((8, 13), F32),
-        ),
-        in_specs=[vmem, hbm, smem, smem, smem, hbm, hbm, hbm],
-        out_specs=(hbm, vmem, hbm, vmem, hbm, vmem),
+        out_shape=(codes, codes, codes, codes, pltpu.VMEM((32, 128), F32)),
+        in_specs=[hbm, hbm, smem, smem, smem, hbm, hbm, hbm],
+        out_specs=(vmem,) * 5,
         scratch_shapes=[
+            pltpu.VMEM((128, 2048), BF16),
             pltpu.VMEM((32, 1024, 128), BF16),
             pltpu.VMEM((1024, 128), BF16),
             pltpu.VMEM((CHUNKS, 4096, 128), BF16),
-            pltpu.VMEM((1024, 1664), BF16),
-            pltpu.VMEM((1024, 1664), BF16),
-            pltpu.VMEM((1024, 1664), BF16),
             pltpu.VMEM((1024, 128), F32),
             pltpu.VMEM((3, 1024, 128), F32),
             pltpu.VMEM((24, 8, 128), F32),
             pltpu.VMEM((24, 128), F32),
-            pltpu.VMEM((24, 128), F32),
-            pltpu.VMEM((8, 128), F32),
-            dma((3,)), dma((CHUNKS,)),
+            dma((4,)), dma((CHUNKS,)),
             dma((4,)), dma((4,)),
             dma((2, 4)), dma((2, 4)),
             dma((4,)), dma((4,)),
@@ -356,18 +385,31 @@
             dma((2, CHUNKS)), dma((2, CHUNKS)),
             dma((CHUNKS,)), dma((CHUNKS,)),
             dma((1,)), dma((1,)),
-            dma((CHUNKS,)), dma((CHUNKS,)), dma((CHUNKS,)),
         ],
         compiler_params=pltpu.CompilerParams(
-            collective_id=0, has_side_effects=True, vmem_limit_bytes=56 << 20
+            collective_id=0, has_side_effects=True, vmem_limit_bytes=32 << 20
         ),
         cost_estimate=pl.CostEstimate(
             flops=2 * 1024 * 1664 * 4096, bytes_accessed=26 << 20, transcendentals=2 * 1024 * 1664
         ),
     )(
-        activations[0], out_grads[0], weight_scale, moment_scale, second_scale,
-        weight_code, moment_code, second_code,
+        pinned(activations[0]), pinned(out_grads[0]),
+        pinned(weight_scale), pinned(moment_scale), pinned(second_scale),
+        pinned(weight_code), pinned(moment_code), pinned(second_code),
     )
+    return pl.pallas_call(
+        store_kernel,
+        out_shape=(
+            shape((2048, 1664), BF16), shape((16, 13), F32),
+            shape((1024, 1664), BF16), shape((8, 13), F32),
+            shape((1024, 1664), BF16), shape((8, 13), F32),
+        ),
+        in_specs=[vmem] * 5,
+        out_specs=(hbm, vmem, hbm, vmem, hbm, vmem),
+        scratch_shapes=[dma((4, 4))],
+        compiler_params=pltpu.CompilerParams(vmem_limit_bytes=8 << 20),
+        cost_estimate=pl.CostEstimate(flops=0, bytes_accessed=26 << 20, transcendentals=0),
+    )(*(pltpu.with_memory_space_constraint(x, pltpu.VMEM) for x in held))
 
 
 def solution(mesh):

time: 160 us -> 140 us (0.88)
  local copies, waits for them, and re-layouts: 12.6 us -> 0 us
  Pallas kernels: 147 us -> 139 us
    unnamed x16 -> x0, local copies, waits for them, and re-layouts: 12.6 us -> none
    pallas_call x1 -> x2, Pallas kernels: 147 us -> 139 us  [the longest x1 133 us: per_device(): pl.pallas_call(kernel, out_shape=(codes, codes, codes, codes, pltpu.VMEM(...]
where the time goes in v2:
time: 140 us; the launch traced here: 139 us
  Pallas kernels  139 us (99%)
    pallas_call x1, Pallas kernels, per_device(): pl.pallas_call(kernel, out_shape=(codes, codes, codes, codes, pltpu.VMEM(...  133 us
    pallas_call x1, Pallas kernels, per_device(): pl.pallas_call(store_kernel, out_shape=(shape((2048, 1664), BF16), shape(...  5.62 us

profile of v2, /device:TPU:0, one launch (start us, length us, event | category | flops | bytes accessed | tf_op | source)
XLA Modules:
  0.0 139.3 jit_solution(7288680282833557199)
XLA Ops:
  0.6 133.0 %shard_map.127 = (bf16[1024,1664]{1,0:T(8,128)(2,1)S(1)}, bf16[1024,1664]{1,0:T(8,128)(2,1)S(1)}, bf16[1024,1664]{1,0:T(8,128)(2,1)S(1)}, bf16[1024,1664]{1,0:T(8,128)(2,1)S(1)}, f32[32,128]{1,0:T(8,128)S(1)}) custom-call(bf16[128,2048]{1,0:T(8,128)(2,1)} %bitcast.3, bf16[512,1664]{1,0:T(8,128)(2,1)} %bitcast.2, f32[8,13]{1,0:T(8,128)} %w_scale.1, ...), custom_call_target="tpu_custom_call" | custom-call | flops 13958643712 | bytes 27262976 | tf_op jit(solution)/shard_map/pallas_call | solution.py:364
  133.6 5.6 %shard_map.128 = (bf16[2048,1664]{1,0:T(8,128)(2,1)}, f32[16,13]{1,0:T(8,128)}, bf16[1024,1664]{1,0:T(8,128)(2,1)}, f32[8,13]{1,0:T(8,128)}, bf16[1024,1664]{1,0:T(8,128)(2,1)}, /*index=5*/f32[8,13]{1,0:T(8,128)}) custom-call(bf16[1024,1664]{1,0:T(8,128)(2,1)S(1)} %get-tuple-element.11.W, bf16[1024,1664]{1,0:T(8,128)(2,1)S(1)} %get-tuple-element.12.peer_w, ...), custom_call_target="tpu_custom_call" | custom-call | bytes 27262976 | tf_op jit(solution)/shard_map/pallas_call | solution.py:400

commit v3 on v2

--- a/solution.py
+++ b/solution.py
@@ -16,9 +16,9 @@
 
 
 def kernel(
-    acts_in, grads, w_scale, m_scale, v_scale, w_code, m_code, v_code,
+    acts_in, grads, w_scale_in, m_scale_in, v_scale_in, w_code, m_code, v_code,
     W, peer_w, M, V, scales,
-    acts, A, T, G, acc, new, peak, inv,
+    acts, A, T, G, acc, new, peak, inv, w_scale, m_scale, v_scale,
     in_sem, own_sem, y_send, y_recv, z_send, z_recv, zf_send, zf_recv, sib_send, sib_recv,
     s1_send, s1_recv, sx_send, sx_recv, s4_send, s4_recv,
     w_send, w_recv, sc_send, sc_recv,
@@ -39,6 +39,10 @@
     z_dev = (at(yh, z_next, k, c, p), at(yh, z_prev, k, c, p))
     x_dev = (at(yh, z, k, c_next, p), at(yh, z, k, c_prev, p))
 
+    barrier = pltpu.get_barrier_semaphore()
+    for device in (partner, other, across, sibling) + z_dev + x_dev:
+        pl.semaphore_signal(barrier, inc=1, device_id=device, device_id_type=MESH)
+
     def remote(src, dst, send, recv, device):
         return pltpu.make_async_remote_copy(
             src_ref=src, dst_ref=dst, send_sem=send, recv_sem=recv,
@@ -63,13 +67,12 @@
         pltpu.make_async_copy(w_code, W, in_sem.at[0]),
         pltpu.make_async_copy(m_code, M, in_sem.at[1]),
         pltpu.make_async_copy(v_code, V, in_sem.at[2]),
+        pltpu.make_async_copy(w_scale_in, w_scale, in_sem.at[4]),
+        pltpu.make_async_copy(m_scale_in, m_scale, in_sem.at[5]),
+        pltpu.make_async_copy(v_scale_in, v_scale, in_sem.at[6]),
     ]
     load_acts = pltpu.make_async_copy(acts_in, acts, in_sem.at[3])
     load_acts.start()
-
-    barrier = pltpu.get_barrier_semaphore()
-    for device in (partner, other, across, sibling) + z_dev + x_dev:
-        pl.semaphore_signal(barrier, inc=1, device_id=device, device_id_type=MESH)
 
     scales[0:24, :] = jnp.zeros((24, 128), F32)
     load_acts.wait()
@@ -166,11 +169,15 @@
     def x_step(j):
         forward(j)
 
-        @pl.when(j < 3)
+        @pl.when(j < CHUNKS - 4)
         def _():
             send_partner(j + 3)
 
-        @pl.when(jnp.logical_and(j > 3, j < CHUNKS - 2))
+        @pl.when(jnp.logical_and(j > 2, j < CHUNKS - 4))
+        def _():
+            send_own(j + 3)
+
+        @pl.when(j == CHUNKS - 3)
         def _():
             send_partner(j + 2)
             send_own(j + 2)
@@ -237,9 +244,9 @@
     finish(0)
     finish(2)
     x_step(3)
+    x_step(4)
     finish(1)
     finish(3)
-    x_step(4)
     for load in loads:
         load.wait()
     for h in range(4):
@@ -251,21 +258,28 @@
     def w_copy(j):
         return remote(W.at[:, cols(j)], peer_w.at[:, cols(j)], w_send.at[j], w_recv.at[j], partner)
 
+    sc_copy = remote(scales.at[0:8], scales.at[24:32], sc_send.at[0], sc_recv.at[0], partner)
+
+    def product(j, c_):
+        left = jnp.concatenate([A[c_ * 8 + i] for i in range(8)], axis=1)
+        right = G[j, pl.ds(pl.multiple_of(c_ * 1024, 1024), 1024), :]
+        return jnp.dot(left, right, preferred_element_type=F32)
+
     def chunk(j, carry):
-        @pl.when(j == 3)
-        def _():
-            x_step(5)
-
-        @pl.when(jnp.logical_and(j > 4, j < CHUNKS - 1))
-        def _():
-            x_step(j + 1)
+        @pl.when(jnp.logical_or(j == 1, j == 3))
+        def _():
+            x_step(5 + j // 2)
+
+        @pl.when(jnp.logical_or(j == 5, jnp.logical_and(j > 6, j < CHUNKS - 1)))
+        def _():
+            x_step(jnp.where(j == 5, 7, j + 1))
 
         sx_landed(j, 1, 0).wait_recv()
         sx_landed(j, 0, 1).wait_recv()
+        acc[...] = product(j, c) + product(j, c_prev) + product(j, c_next)
         s4_landed(j, 0).wait_recv()
         s4_landed(j, 1).wait_recv()
-        left = jnp.concatenate([A[i] for i in range(32)], axis=1)
-        acc[...] = jnp.dot(left, G[j], preferred_element_type=F32)
+        acc[...] += product(j, c_far)
 
         def update(d, carry):
             rows = pl.ds(pl.multiple_of(d * 128, 128), 128)
@@ -289,6 +303,10 @@
         scales[0:24, :] = jnp.where(lane == j, scale, scales[0:24, :])
         inv[...] = 1.0 / scale
 
+        @pl.when(j == CHUNKS - 1)
+        def _():
+            sc_copy.start()
+
         def encode(d, carry):
             rows = pl.ds(pl.multiple_of(d * 128, 128), 128)
             for n, out in enumerate((W, M, V)):
@@ -300,9 +318,6 @@
         return carry
 
     lax.fori_loop(0, CHUNKS, chunk, 0)
-
-    sc_copy = remote(scales.at[0:8], scales.at[24:32], sc_send.at[0], sc_recv.at[0], partner)
-    sc_copy.start()
 
     for i in (1, 2, 3):
         y_copy(i).wait_send()
@@ -326,7 +341,7 @@
     sc_copy.wait()
 
 
-def store_kernel(W, peer_w, M, V, scales, w_out, ws_out, m_out, ms_out, v_out, vs_out, sem):
+def store_kernel(W, peer_w, M, V, scales, w_out, ws_out, m_out, ms_out, v_out, vs_out, ws, ms, vs, sem, sc_sem):
     p = lax.axis_index("rep")
     q = 1 - p
     copies = []
@@ -342,10 +357,13 @@
         ]
     for copy in copies:
         copy.start()
-    ws_out[pl.ds(pl.multiple_of(p * 8, 8), 8), :] = scales[0:8, :CHUNKS]
-    ws_out[pl.ds(pl.multiple_of(q * 8, 8), 8), :] = scales[24:32, :CHUNKS]
-    ms_out[...] = scales[8:16, :CHUNKS]
-    vs_out[...] = scales[16:24, :CHUNKS]
+    ws[pl.ds(pl.multiple_of(p * 8, 8), 8), :] = scales[0:8, :CHUNKS]
+    ws[pl.ds(pl.multiple_of(q * 8, 8), 8), :] = scales[24:32, :CHUNKS]
+    ms[...] = scales[8:16, :CHUNKS]
+    vs[...] = scales[16:24, :CHUNKS]
+    for n, (src, dst) in enumerate(((ws, ws_out), (ms, ms_out), (vs, vs_out))):
+        copies.append(pltpu.make_async_copy(src, dst, sc_sem.at[n]))
+        copies[-1].start()
     for copy in copies:
         copy.wait()
 
@@ -355,7 +373,6 @@
     moment_code, moment_scale, second_code, second_scale,
 ):
     vmem = pl.BlockSpec(memory_space=pltpu.VMEM)
-    smem = pl.BlockSpec(memory_space=pltpu.SMEM)
     hbm = pl.BlockSpec(memory_space=pl.ANY)
     dma = pltpu.SemaphoreType.DMA
     shape = jax.ShapeDtypeStruct
@@ -364,7 +381,7 @@
     held = pl.pallas_call(
         kernel,
         out_shape=(codes, codes, codes, codes, pltpu.VMEM((32, 128), F32)),
-        in_specs=[hbm, hbm, smem, smem, smem, hbm, hbm, hbm],
+        in_specs=[hbm] * 8,
         out_specs=(vmem,) * 5,
         scratch_shapes=[
             pltpu.VMEM((128, 2048), BF16),
@@ -375,7 +392,10 @@
             pltpu.VMEM((3, 1024, 128), F32),
             pltpu.VMEM((24, 8, 128), F32),
             pltpu.VMEM((24, 128), F32),
-            dma((4,)), dma((CHUNKS,)),
+            pltpu.SMEM((8, 13), F32),
+            pltpu.SMEM((8, 13), F32),
+            pltpu.SMEM((8, 13), F32),
+            dma((7,)), dma((CHUNKS,)),
             dma((4,)), dma((4,)),
             dma((2, 4)), dma((2, 4)),
             dma((4,)), dma((4,)),
@@ -405,8 +425,11 @@
             shape((1024, 1664), BF16), shape((8, 13), F32),
         ),
         in_specs=[vmem] * 5,
-        out_specs=(hbm, vmem, hbm, vmem, hbm, vmem),
-        scratch_shapes=[dma((4, 4))],
+        out_specs=(hbm,) * 6,
+        scratch_shapes=[
+            pltpu.VMEM((16, 13), F32), pltpu.VMEM((8, 13), F32), pltpu.VMEM((8, 13), F32),
+            dma((4, 4)), dma((3,)),
+        ],
         compiler_params=pltpu.CompilerParams(vmem_limit_bytes=8 << 20),
         cost_estimate=pl.CostEstimate(flops=0, bytes_accessed=26 << 20, transcendentals=0),
     )(*(pltpu.with_memory_space_constraint(x, pltpu.VMEM) for x in held))

time: 140 us -> 138 us (0.986)
  Pallas kernels: 139 us -> 137 us
where the time goes in v3:
time: 138 us
  Pallas kernels  137 us (99%)
    pallas_call x1, Pallas kernels, per_device(): pl.pallas_call(kernel, out_shape=(codes, codes, codes, codes, pltpu.VMEM(...  132 us
    pallas_call x1, Pallas kernels, per_device(): pl.pallas_call(store_kernel, out_shape=(shape((2048, 1664), BF16), shape(...  5.05 us

profile of v3, /device:TPU:0, one launch (start us, length us, event | category | flops | bytes accessed | tf_op | source)
XLA Modules:
  0.0 137.9 jit_solution(596039548150174911)
XLA Ops:
  0.6 132.2 %shard_map.127 = (bf16[1024,1664]{1,0:T(8,128)(2,1)S(1)}, bf16[1024,1664]{1,0:T(8,128)(2,1)S(1)}, bf16[1024,1664]{1,0:T(8,128)(2,1)S(1)}, bf16[1024,1664]{1,0:T(8,128)(2,1)S(1)}, f32[32,128]{1,0:T(8,128)S(1)}) custom-call(bf16[128,2048]{1,0:T(8,128)(2,1)} %bitcast.3, bf16[512,1664]{1,0:T(8,128)(2,1)} %bitcast.2, f32[8,13]{1,0:T(8,128)} %w_scale_in.1, ...), custom_call_target="tpu_custom_call" | custom-call | flops 13958643712 | bytes 27262976 | tf_op jit(solution)/shard_map/pallas_call | solution.py:381
  132.9 5.0 %shard_map.128 = (bf16[2048,1664]{1,0:T(8,128)(2,1)}, f32[16,13]{1,0:T(8,128)}, bf16[1024,1664]{1,0:T(8,128)(2,1)}, f32[8,13]{1,0:T(8,128)}, bf16[1024,1664]{1,0:T(8,128)(2,1)}, /*index=5*/f32[8,13]{1,0:T(8,128)}) custom-call(bf16[1024,1664]{1,0:T(8,128)(2,1)S(1)} %get-tuple-element.11.W, bf16[1024,1664]{1,0:T(8,128)(2,1)S(1)} %get-tuple-element.12.peer_w, ...), custom_call_target="tpu_custom_call" | custom-call | bytes 27262976 | tf_op jit(solution)/shard_map/pallas_call | solution.py:420

commit v4 on v3

--- a/solution.py
+++ b/solution.py
@@ -19,9 +19,8 @@
     acts_in, grads, w_scale_in, m_scale_in, v_scale_in, w_code, m_code, v_code,
     W, peer_w, M, V, scales,
     acts, A, T, G, acc, new, peak, inv, w_scale, m_scale, v_scale,
-    in_sem, own_sem, y_send, y_recv, z_send, z_recv, zf_send, zf_recv, sib_send, sib_recv,
-    s1_send, s1_recv, sx_send, sx_recv, s4_send, s4_recv,
-    w_send, w_recv, sc_send, sc_recv,
+    in_sem, own_sem, y_recv, z_recv, zf_recv, sib_recv,
+    s1_recv, direct_recv, near_recv, far_recv, w_recv, sc_recv, a_send, g_send, w_send, sc_send,
 ):
     r, c, p = lax.axis_index("row"), lax.axis_index("col"), lax.axis_index("rep")
     yh, z, k = r // 8, (r // 2) % 4, r % 2
@@ -56,7 +55,7 @@
         return pl.ds(pl.multiple_of(j * 128, 128), 128)
 
     def load_own(j):
-        return pltpu.make_async_copy(grads.at[:, cols(j)], G.at[j, own_rows(p, c)], own_sem.at[j])
+        return pltpu.make_async_copy(grads.at[:, cols(j)], G.at[j, own_rows(p, c)], own_sem.at[0])
 
     def start_own(j, carry):
         load_own(j).start()
@@ -95,61 +94,58 @@
 
     def y_copy(i):
         src = A.at[mine] if i == 3 else T
-        return remote(src, A.at[mine], y_send.at[i], y_recv.at[i], (None, partner, other, across)[i])
+        return remote(src, A.at[mine], a_send.at[0], y_recv.at[i], (None, partner, other, across)[i])
 
     def y_landed(i):
         got = piece(i, z, k)
-        return remote(got, got, y_send.at[i], y_recv.at[i], (None, partner, other, across)[i])
+        return remote(got, got, a_send.at[0], y_recv.at[i], (None, partner, other, across)[i])
 
     def z_copy(i, d):
-        return remote(piece(i, z, k), piece(i, z, k), z_send.at[d, i], z_recv.at[d, i], z_dev[d])
-
-    def z_landed(i, d):
-        got = piece(i, (z_prev, z_next)[d], k)
-        return remote(got, got, z_send.at[d, i], z_recv.at[d, i], z_dev[d])
+        return remote(piece(i, z, k), piece(i, z, k), a_send.at[0], z_recv.at[i], z_dev[d])
+
+    def z_landed(i):
+        both = A.at[0:2]
+        return remote(both, both, a_send.at[0], z_recv.at[i], z_dev[0])
 
     def zf_copy(i):
         d = i // 2
         got = piece(i, (z_prev, z_next)[d], k)
-        return remote(got, got, zf_send.at[i], zf_recv.at[i], z_dev[d])
+        return remote(got, got, a_send.at[0], zf_recv.at[i], z_dev[d])
 
     def zf_landed(i):
         got = piece(i, z_far, k)
-        return remote(got, got, zf_send.at[i], zf_recv.at[i], z_dev[i // 2])
+        return remote(got, got, a_send.at[0], zf_recv.at[i], z_dev[i // 2])
 
     hops = (z, z_prev, z_next, z_far)
 
     def sib_copy(i, h):
         got = piece(i, hops[h], k)
-        return remote(got, got, sib_send.at[h, i], sib_recv.at[h, i], sibling)
-
-    def sib_landed(i, h):
-        got = piece(i, hops[h], 1 - k)
-        return remote(got, got, sib_send.at[h, i], sib_recv.at[h, i], sibling)
+        return remote(got, got, a_send.at[0], sib_recv.at[0], sibling)
+
+    def sib_landed():
+        every = A.at[0:16]
+        return remote(every, every, a_send.at[0], sib_recv.at[0], sibling)
 
     def s1_copy(j):
         rows = G.at[j, own_rows(p, c)]
-        return remote(rows, rows, s1_send.at[j], s1_recv.at[j], partner)
+        return remote(rows, rows, g_send.at[0], s1_recv.at[j], partner)
 
     def s1_landed(j):
         rows = G.at[j, own_rows(q, c)]
-        return remote(rows, rows, s1_send.at[j], s1_recv.at[j], partner)
+        return remote(rows, rows, g_send.at[0], s1_recv.at[j], partner)
 
     def sx_copy(j, part, d):
         rows = G.at[j, own_rows((p, q)[part], c)]
-        return remote(rows, rows, sx_send.at[part, d, j], sx_recv.at[part, d, j], x_dev[d])
-
-    def sx_landed(j, part, d):
-        rows = G.at[j, own_rows((p, q)[part], (c_prev, c_next)[d])]
-        return remote(rows, rows, sx_send.at[part, d, j], sx_recv.at[part, d, j], x_dev[d])
+        recv = direct_recv if part == d else near_recv
+        return remote(rows, rows, g_send.at[0], recv.at[j], x_dev[d])
 
     def s4_copy(j, d):
         rows = G.at[j, own_rows((p, q)[d], (c_prev, c_next)[d])]
-        return remote(rows, rows, s4_send.at[d, j], s4_recv.at[d, j], x_dev[d])
-
-    def s4_landed(j, d):
-        rows = G.at[j, own_rows((p, q)[d], c_far)]
-        return remote(rows, rows, s4_send.at[d, j], s4_recv.at[d, j], x_dev[d])
+        return remote(rows, rows, g_send.at[0], far_recv.at[j], x_dev[d])
+
+    def pair_landed(j, recv):
+        both = G.at[j, 0:1024]
+        return remote(both, both, g_send.at[0], recv.at[j], x_dev[0])
 
     def send_own(j):
         sx_copy(j, 0, 0).start()
@@ -161,35 +157,26 @@
         sx_copy(j, 1, 1).start()
 
     def forward(j):
-        sx_landed(j, 0, 0).wait_recv()
+        pair_landed(j, direct_recv).wait_recv()
         s4_copy(j, 0).start()
-        sx_landed(j, 1, 1).wait_recv()
         s4_copy(j, 1).start()
 
     def x_step(j):
         forward(j)
 
-        @pl.when(j < CHUNKS - 4)
+        @pl.when(j < 3)
         def _():
             send_partner(j + 3)
 
-        @pl.when(jnp.logical_and(j > 2, j < CHUNKS - 4))
-        def _():
-            send_own(j + 3)
-
-        @pl.when(j == CHUNKS - 3)
+        @pl.when(jnp.logical_and(j > 3, j < CHUNKS - 2))
         def _():
             send_partner(j + 2)
             send_own(j + 2)
 
     def relay(i):
-        z_landed(i, 0).wait_recv()
-        if i < 2:
-            zf_copy(i).start()
+        z_landed(i).wait_recv()
+        zf_copy(i).start()
         sib_copy(i, 1).start()
-        z_landed(i, 1).wait_recv()
-        if i >= 2:
-            zf_copy(i).start()
         sib_copy(i, 2).start()
 
     def spread(i):
@@ -207,11 +194,8 @@
     z_copy(0, 0).start()
     z_copy(0, 1).start()
 
-    def wait_own(j, carry):
-        load_own(j).wait()
-        return carry
-
-    lax.fori_loop(0, CHUNKS, wait_own, 0)
+    own = G.at[:, own_rows(p, c)]
+    pltpu.make_async_copy(own, own, own_sem.at[0]).wait()
 
     def start_own_sends(j, carry):
         send_own(j)
@@ -249,14 +233,12 @@
     finish(3)
     for load in loads:
         load.wait()
-    for h in range(4):
-        for i in range(4):
-            sib_landed(i, h).wait_recv()
+    sib_landed().wait_recv()
 
     lane = lax.broadcasted_iota(jnp.int32, (24, 128), 1)
 
     def w_copy(j):
-        return remote(W.at[:, cols(j)], peer_w.at[:, cols(j)], w_send.at[j], w_recv.at[j], partner)
+        return remote(W.at[:, cols(j)], peer_w.at[:, cols(j)], w_send.at[0], w_recv.at[0], partner)
 
     sc_copy = remote(scales.at[0:8], scales.at[24:32], sc_send.at[0], sc_recv.at[0], partner)
 
@@ -274,11 +256,9 @@
         def _():
             x_step(jnp.where(j == 5, 7, j + 1))
 
-        sx_landed(j, 1, 0).wait_recv()
-        sx_landed(j, 0, 1).wait_recv()
+        pair_landed(j, near_recv).wait_recv()
         acc[...] = product(j, c) + product(j, c_prev) + product(j, c_next)
-        s4_landed(j, 0).wait_recv()
-        s4_landed(j, 1).wait_recv()
+        pair_landed(j, far_recv).wait_recv()
         acc[...] += product(j, c_far)
 
         def update(d, carry):
@@ -319,25 +299,13 @@
 
     lax.fori_loop(0, CHUNKS, chunk, 0)
 
-    for i in (1, 2, 3):
-        y_copy(i).wait_send()
-    for i in range(4):
-        z_copy(i, 0).wait_send()
-        z_copy(i, 1).wait_send()
-        zf_copy(i).wait_send()
-        for h in range(4):
-            sib_copy(i, h).wait_send()
-
-    def drain(j, carry):
-        s1_copy(j).wait_send()
-        for d in range(2):
-            sx_copy(j, 0, d).wait_send()
-            sx_copy(j, 1, d).wait_send()
-            s4_copy(j, d).wait_send()
-        w_copy(j).wait()
-        return carry
-
-    lax.fori_loop(0, CHUNKS, drain, 0)
+    sent = A.at[0:31]
+    remote(sent, sent, a_send.at[0], sib_recv.at[0], sibling).wait_send()
+    sent = G.at[:, 0:3584]
+    remote(sent, sent, g_send.at[0], s1_recv.at[0], partner).wait_send()
+    codes = remote(W, peer_w, w_send.at[0], w_recv.at[0], partner)
+    codes.wait_send()
+    codes.wait_recv()
     sc_copy.wait()
 
 
@@ -395,16 +363,9 @@
             pltpu.SMEM((8, 13), F32),
             pltpu.SMEM((8, 13), F32),
             pltpu.SMEM((8, 13), F32),
-            dma((7,)), dma((CHUNKS,)),
-            dma((4,)), dma((4,)),
-            dma((2, 4)), dma((2, 4)),
-            dma((4,)), dma((4,)),
-            dma((4, 4)), dma((4, 4)),
-            dma((CHUNKS,)), dma((CHUNKS,)),
-            dma((2, 2, CHUNKS)), dma((2, 2, CHUNKS)),
-            dma((2, CHUNKS)), dma((2, CHUNKS)),
-            dma((CHUNKS,)), dma((CHUNKS,)),
-            dma((1,)), dma((1,)),
+            dma((7,)), dma((1,)), dma((4,)), dma((4,)), dma((4,)), dma((1,)),
+            dma((CHUNKS,)), dma((CHUNKS,)), dma((CHUNKS,)), dma((CHUNKS,)), dma((1,)), dma((1,)),
+            dma((1,)), dma((1,)), dma((1,)), dma((1,)),
         ],
         compiler_params=pltpu.CompilerParams(
             collective_id=0, has_side_effects=True, vmem_limit_bytes=32 << 20

time: 138 us -> 136 us (0.986)
  Pallas kernels: 137 us -> 135 us
    pallas_call x1, Pallas kernels: 132 us -> 130 us  [per_device(): pl.pallas_call(kernel, out_shape=(codes, codes, codes, codes, pltpu.VMEM(...]
where the time goes in v4:
time: 136 us
  Pallas kernels  135 us (99%)
    pallas_call x1, Pallas kernels, per_device(): pl.pallas_call(kernel, out_shape=(codes, codes, codes, codes, pltpu.VMEM(...  130 us
    pallas_call x1, Pallas kernels, per_device(): pl.pallas_call(store_kernel, out_shape=(shape((2048, 1664), BF16), shape(...  5.05 us

profile of v4, /device:TPU:0, one launch (start us, length us, event | category | flops | bytes accessed | tf_op | source)
XLA Modules:
  0.0 135.7 jit_solution(7958766269047825598)
XLA Ops:
  0.6 130.0 %shard_map.127 = (bf16[1024,1664]{1,0:T(8,128)(2,1)S(1)}, bf16[1024,1664]{1,0:T(8,128)(2,1)S(1)}, bf16[1024,1664]{1,0:T(8,128)(2,1)S(1)}, bf16[1024,1664]{1,0:T(8,128)(2,1)S(1)}, f32[32,128]{1,0:T(8,128)S(1)}) custom-call(bf16[128,2048]{1,0:T(8,128)(2,1)} %bitcast.3, bf16[512,1664]{1,0:T(8,128)(2,1)} %bitcast.2, f32[8,13]{1,0:T(8,128)} %w_scale_in.1, ...), custom_call_target="tpu_custom_call" | custom-call | flops 13958643712 | bytes 27262976 | tf_op jit(solution)/shard_map/pallas_call | solution.py:349
  130.7 5.0 %shard_map.128 = (bf16[2048,1664]{1,0:T(8,128)(2,1)}, f32[16,13]{1,0:T(8,128)}, bf16[1024,1664]{1,0:T(8,128)(2,1)}, f32[8,13]{1,0:T(8,128)}, bf16[1024,1664]{1,0:T(8,128)(2,1)}, /*index=5*/f32[8,13]{1,0:T(8,128)}) custom-call(bf16[1024,1664]{1,0:T(8,128)(2,1)S(1)} %get-tuple-element.11.W, bf16[1024,1664]{1,0:T(8,128)(2,1)S(1)} %get-tuple-element.12.peer_w, ...), custom_call_target="tpu_custom_call" | custom-call | bytes 27262976 | tf_op jit(solution)/shard_map/pallas_call | solution.py:381

commit v5 on v4

--- a/solution.py
+++ b/solution.py
@@ -57,6 +57,9 @@
     def load_own(j):
         return pltpu.make_async_copy(grads.at[:, cols(j)], G.at[j, own_rows(p, c)], own_sem.at[0])
 
+    load_acts = pltpu.make_async_copy(acts_in, acts, in_sem.at[3])
+    load_acts.start()
+
     def start_own(j, carry):
         load_own(j).start()
         return carry
@@ -70,8 +73,6 @@
         pltpu.make_async_copy(m_scale_in, m_scale, in_sem.at[5]),
         pltpu.make_async_copy(v_scale_in, v_scale, in_sem.at[6]),
     ]
-    load_acts = pltpu.make_async_copy(acts_in, acts, in_sem.at[3])
-    load_acts.start()
 
     scales[0:24, :] = jnp.zeros((24, 128), F32)
     load_acts.wait()
@@ -156,6 +157,14 @@
         sx_copy(j, 1, 0).start()
         sx_copy(j, 1, 1).start()
 
+    def send_direct(j):
+        sx_copy(j, 0, 0).start()
+        sx_copy(j, 1, 1).start()
+
+    def send_near(j):
+        sx_copy(j, 1, 0).start()
+        sx_copy(j, 0, 1).start()
+
     def forward(j):
         pair_landed(j, direct_recv).wait_recv()
         s4_copy(j, 0).start()
@@ -170,8 +179,16 @@
 
         @pl.when(jnp.logical_and(j > 3, j < CHUNKS - 2))
         def _():
-            send_partner(j + 2)
-            send_own(j + 2)
+            s1_landed(j + 2).wait_recv()
+            send_direct(j + 2)
+
+        @pl.when(jnp.logical_and(j > 3, j < CHUNKS - 3))
+        def _():
+            send_near(j + 2)
+
+        @pl.when(j == CHUNKS - 2)
+        def _():
+            send_near(j + 1)
 
     def relay(i):
         z_landed(i).wait_recv()
@@ -191,17 +208,18 @@
 
     for i in (1, 2, 3):
         y_copy(i).start()
+    own = G.at[:, own_rows(p, c)]
+    pltpu.make_async_copy(own, own, own_sem.at[0]).wait()
+
+    send_own(0)
     z_copy(0, 0).start()
     z_copy(0, 1).start()
-
-    own = G.at[:, own_rows(p, c)]
-    pltpu.make_async_copy(own, own, own_sem.at[0]).wait()
 
     def start_own_sends(j, carry):
         send_own(j)
         return carry
 
-    lax.fori_loop(0, 6, start_own_sends, 0)
+    lax.fori_loop(1, 6, start_own_sends, 0)
 
     def start_s1(j, carry):
         s1_copy(j).start()

time: 136 us -> 134 us (0.985)
  Pallas kernels: 135 us -> 133 us
    pallas_call x1, Pallas kernels: 130 us -> 128 us  [per_device(): pl.pallas_call(kernel, out_shape=(codes, codes, codes, codes, pltpu.VMEM(...]
where the time goes in v5:
time: 134 us
  Pallas kernels  133 us (99%)
    pallas_call x1, Pallas kernels, per_device(): pl.pallas_call(kernel, out_shape=(codes, codes, codes, codes, pltpu.VMEM(...  128 us
    pallas_call x1, Pallas kernels, per_device(): pl.pallas_call(store_kernel, out_shape=(shape((2048, 1664), BF16), shape(...  5.05 us

profile of v5, /device:TPU:0, one launch (start us, length us, event | category | flops | bytes accessed | tf_op | source)
XLA Modules:
  0.0 133.8 jit_solution(7114898657697885431)
XLA Ops:
  0.6 128.1 %shard_map.127 = (bf16[1024,1664]{1,0:T(8,128)(2,1)S(1)}, bf16[1024,1664]{1,0:T(8,128)(2,1)S(1)}, bf16[1024,1664]{1,0:T(8,128)(2,1)S(1)}, bf16[1024,1664]{1,0:T(8,128)(2,1)S(1)}, f32[32,128]{1,0:T(8,128)S(1)}) custom-call(bf16[128,2048]{1,0:T(8,128)(2,1)} %bitcast.3, bf16[512,1664]{1,0:T(8,128)(2,1)} %bitcast.2, f32[8,13]{1,0:T(8,128)} %w_scale_in.1, ...), custom_call_target="tpu_custom_call" | custom-call | flops 13958643712 | bytes 27262976 | tf_op jit(solution)/shard_map/pallas_call | solution.py:367
  128.8 5.0 %shard_map.128 = (bf16[2048,1664]{1,0:T(8,128)(2,1)}, f32[16,13]{1,0:T(8,128)}, bf16[1024,1664]{1,0:T(8,128)(2,1)}, f32[8,13]{1,0:T(8,128)}, bf16[1024,1664]{1,0:T(8,128)(2,1)}, /*index=5*/f32[8,13]{1,0:T(8,128)}) custom-call(bf16[1024,1664]{1,0:T(8,128)(2,1)S(1)} %get-tuple-element.11.W, bf16[1024,1664]{1,0:T(8,128)(2,1)S(1)} %get-tuple-element.12.peer_w, ...), custom_call_target="tpu_custom_call" | custom-call | bytes 27262976 | tf_op jit(solution)/shard_map/pallas_call | solution.py:399

commit v6 on v5

--- a/solution.py
+++ b/solution.py
@@ -11,13 +11,14 @@
 F32 = jnp.float32
 BF16 = jnp.bfloat16
 CHUNKS = 13
+MOST = 12 * 128
 BIAS_ONE = 1.0 - 0.9**10
 BIAS_TWO = 1.0 - 0.95**10
 
 
 def kernel(
     acts_in, grads, w_scale_in, m_scale_in, v_scale_in, w_code, m_code, v_code,
-    W, peer_w, M, V, scales,
+    W, peer_w, M, V, scales, last,
     acts, A, T, G, acc, new, peak, inv, w_scale, m_scale, v_scale,
     in_sem, own_sem, y_recv, z_recv, zf_recv, sib_recv,
     s1_recv, direct_recv, near_recv, far_recv, w_recv, sc_recv, a_send, g_send, w_send, sc_send,
@@ -260,6 +261,8 @@
 
     sc_copy = remote(scales.at[0:8], scales.at[24:32], sc_send.at[0], sc_recv.at[0], partner)
 
+    keep_last = pltpu.make_async_copy(W.at[:, MOST:], last, in_sem.at[3])
+
     def product(j, c_):
         left = jnp.concatenate([A[c_ * 8 + i] for i in range(8)], axis=1)
         right = G[j, pl.ds(pl.multiple_of(c_ * 1024, 1024), 1024), :]
@@ -312,7 +315,14 @@
             return carry
 
         lax.fori_loop(0, 8, encode, 0)
-        w_copy(j).start()
+        @pl.when(j < CHUNKS - 1)
+        def _():
+            w_copy(j).start()
+
+        @pl.when(j == CHUNKS - 1)
+        def _():
+            keep_last.start()
+
         return carry
 
     lax.fori_loop(0, CHUNKS, chunk, 0)
@@ -321,7 +331,8 @@
     remote(sent, sent, a_send.at[0], sib_recv.at[0], sibling).wait_send()
     sent = G.at[:, 0:3584]
     remote(sent, sent, g_send.at[0], s1_recv.at[0], partner).wait_send()
-    codes = remote(W, peer_w, w_send.at[0], w_recv.at[0], partner)
+    keep_last.wait()
+    codes = remote(W.at[:, :MOST], peer_w.at[:, :MOST], w_send.at[0], w_recv.at[0], partner)
     codes.wait_send()
     codes.wait_recv()
     sc_copy.wait()
@@ -337,7 +348,7 @@
         there = pl.ds(pl.multiple_of(q * 1024 + n * 256, 256), 256)
         copies += [
             pltpu.make_async_copy(W.at[rows], w_out.at[here], sem.at[0, n]),
-            pltpu.make_async_copy(peer_w.at[rows], w_out.at[there], sem.at[1, n]),
+            pltpu.make_async_copy(peer_w.at[rows, :MOST], w_out.at[there, :MOST], sem.at[1, n]),
             pltpu.make_async_copy(M.at[rows], m_out.at[rows], sem.at[2, n]),
             pltpu.make_async_copy(V.at[rows], v_out.at[rows], sem.at[3, n]),
         ]
@@ -354,6 +365,13 @@
         copy.wait()
 
 
+def last_kernel(_, peer_last, w_out, sem):
+    there = pl.ds(pl.multiple_of((1 - lax.axis_index("rep")) * 1024, 1024), 1024)
+    copy = pltpu.make_async_copy(peer_last, w_out.at[there, MOST:], sem.at[0])
+    copy.start()
+    copy.wait()
+
+
 def per_device(
     activations, out_grads, weight_code, weight_scale,
     moment_code, moment_scale, second_code, second_scale,
@@ -364,11 +382,11 @@
     shape = jax.ShapeDtypeStruct
     pinned = functools.partial(pltpu.with_memory_space_constraint, memory_space=pltpu.HBM)
     codes = pltpu.VMEM((1024, 1664), BF16)
-    held = pl.pallas_call(
+    *held, last = pl.pallas_call(
         kernel,
-        out_shape=(codes, codes, codes, codes, pltpu.VMEM((32, 128), F32)),
+        out_shape=(codes, codes, codes, codes, pltpu.VMEM((32, 128), F32), shape((1024, 128), BF16)),
         in_specs=[hbm] * 8,
-        out_specs=(vmem,) * 5,
+        out_specs=(vmem,) * 5 + (hbm,),
         scratch_shapes=[
             pltpu.VMEM((128, 2048), BF16),
             pltpu.VMEM((32, 1024, 128), BF16),
@@ -396,7 +414,8 @@
         pinned(weight_scale), pinned(moment_scale), pinned(second_scale),
         pinned(weight_code), pinned(moment_code), pinned(second_code),
     )
-    return pl.pallas_call(
+    peer_last = lax.ppermute(last, "rep", [(0, 1), (1, 0)])
+    new_w, *rest = pl.pallas_call(
         store_kernel,
         out_shape=(
             shape((2048, 1664), BF16), shape((16, 13), F32),
@@ -412,6 +431,16 @@
         compiler_params=pltpu.CompilerParams(vmem_limit_bytes=8 << 20),
         cost_estimate=pl.CostEstimate(flops=0, bytes_accessed=26 << 20, transcendentals=0),
     )(*(pltpu.with_memory_space_constraint(x, pltpu.VMEM) for x in held))
+    new_w = pl.pallas_call(
+        last_kernel,
+        out_shape=shape((2048, 1664), BF16),
+        in_specs=[hbm, vmem],
+        out_specs=hbm,
+        input_output_aliases={0: 0},
+        scratch_shapes=[dma((1,))],
+        compiler_params=pltpu.CompilerParams(vmem_limit_bytes=8 << 20),
+    )(new_w, peer_last)
+    return (new_w, *rest)
 
 
 def solution(mesh):

time: 134 us -> 132 us (0.985)
  Pallas kernels: 133 us -> 130 us
    pallas_call x1, Pallas kernels: 128 us -> 124 us  [per_device(): pl.pallas_call(kernel, out_shape=(codes, codes, codes, codes, pltpu.VMEM(...]
  transfers between devices with their start and end apart: 0 -> 1, of which waited for: 0 -> 1; matrix products, arithmetic and copies ran while one was open for 0% -> 0% of each run, Pallas kernels for 0% -> 4%
where the time goes in v6:
time: 132 us
  Pallas kernels  130 us (98%)
    pallas_call x1, Pallas kernels, per_device(): pl.pallas_call(kernel, out_shape=(codes, codes, codes, codes, pltpu.VMEM(...  124 us
    pallas_call x1, Pallas kernels, per_device(): pl.pallas_call(store_kernel, out_shape=(shape((2048, 1664), BF16), shape(...  4.96 us
  transfers between devices with their start and end apart: 1, of which 1 were waited for; matrix products, arithmetic and copies ran while one was open for 0% of the time, Pallas kernels for 4%

profile of v6, /device:TPU:0, one launch (start us, length us, event | category | flops | bytes accessed | tf_op | source)
XLA Modules:
  0.0 131.7 jit_solution(16466405093627247926)
XLA Ops:
  0.6 123.9 %shard_map.127 = (bf16[1024,1664]{1,0:T(8,128)(2,1)S(1)}, bf16[1024,1664]{1,0:T(8,128)(2,1)S(1)}, bf16[1024,1664]{1,0:T(8,128)(2,1)S(1)}, bf16[1024,1664]{1,0:T(...) custom-call(bf16[128,2048]{1,0:T(8,128)(2,1)} %bitcast.3, bf16[512,1664]{1,0:T(8,128)(2,1)} %bitcast.2, ...), custom_call_target="tpu_custom_call" | custom-call | flops 13958643712 | bytes 27262976 | tf_op jit(solution)/shard_map/pallas_call | solution.py:385
  124.6 0.8 collective-permute-start
  125.3 5.0 %shard_map.128 = (bf16[2048,1664]{1,0:T(8,128)(2,1)}, f32[16,13]{1,0:T(8,128)}, bf16[1024,1664]{1,0:T(8,128)(2,1)}, f32[8,13]{1,0:T(8,128)}, bf16[1024,1664]{1,0:T(8,128)(2,1)}, /*index=5*/f32[8,13]{1,0:T(8,128)}) custom-call(bf16[1024,1664]{1,0:T(8,128)(2,1)S(1)} %get-tuple-element.18.W, bf16[1024,1664]{1,0:T(8,128)(2,1)S(1)} %get-tuple-element.19.peer_w, ...), custom_call_target="tpu_custom_call" | custom-call | bytes 27262976 | tf_op jit(solution)/shard_map/pallas_call | solution.py:418
  130.3 0.7 collective-permute-done.peer_last
  131.0 0.7 shard_map.129
Async XLA Ops:
  124.6 6.5 %collective-permute-start = (bf16[1024,128]{1,0:T(8,128)(2,1)S(1)}, bf16[1024,128]{1,0:T(8,128)(2,1)S(1)}, u32[]{:S(2)}, u32[]{:S(2)}) collective-permute-start(bf16[1024,128]{1,0:T(8,128)(2,1)S(1)} %get-tuple-element.24), channel_id=1, source_target_pairs={{0,1},{1,0},{2,3},{3,2},{4,5},{5,4},{6,7},{7,6},{8,9},{9,8},{10,11... | collective-permute-start | bytes 786440 | tf_op jit(solution)/shard_map/ppermute | solution.py:417

commit v7 on v6

--- a/solution.py
+++ b/solution.py
@@ -235,8 +235,8 @@
     spread(2)
     relay(0)
     spread(3)
+    send_partner(0)
     relay(1)
-    send_partner(0)
     send_partner(1)
     relay(2)
     send_partner(2)
@@ -244,9 +244,9 @@
     x_step(1)
     x_step(2)
     relay(3)
+    x_step(3)
     finish(0)
     finish(2)
-    x_step(3)
     x_step(4)
     finish(1)
     finish(3)
@@ -269,7 +269,7 @@
         return jnp.dot(left, right, preferred_element_type=F32)
 
     def chunk(j, carry):
-        @pl.when(jnp.logical_or(j == 1, j == 3))
+        @pl.when(jnp.logical_or(j == 0, j == 3))
         def _():
             x_step(5 + j // 2)
 
@@ -342,10 +342,10 @@
     p = lax.axis_index("rep")
     q = 1 - p
     copies = []
-    for n in range(4):
-        rows = pl.ds(n * 256, 256)
-        here = pl.ds(pl.multiple_of(p * 1024 + n * 256, 256), 256)
-        there = pl.ds(pl.multiple_of(q * 1024 + n * 256, 256), 256)
+    for n in range(1):
+        rows = pl.ds(n * 1024, 1024)
+        here = pl.ds(pl.multiple_of(p * 1024 + n * 1024, 1024), 1024)
+        there = pl.ds(pl.multiple_of(q * 1024 + n * 1024, 1024), 1024)
         copies += [
             pltpu.make_async_copy(W.at[rows], w_out.at[here], sem.at[0, n]),
             pltpu.make_async_copy(peer_w.at[rows, :MOST], w_out.at[there, :MOST], sem.at[1, n]),
@@ -426,7 +426,7 @@
         out_specs=(hbm,) * 6,
         scratch_shapes=[
             pltpu.VMEM((16, 13), F32), pltpu.VMEM((8, 13), F32), pltpu.VMEM((8, 13), F32),
-            dma((4, 4)), dma((3,)),
+            dma((4, 1)), dma((3,)),
         ],
         compiler_params=pltpu.CompilerParams(vmem_limit_bytes=8 << 20),
         cost_estimate=pl.CostEstimate(flops=0, bytes_accessed=26 << 20, transcendentals=0),

time: 132 us -> 132 us (level)
  no operation moved by 1% of the time
where the time goes in v7:
time: 132 us
  Pallas kernels  130 us (98%)
    pallas_call x1, Pallas kernels, per_device(): pl.pallas_call(kernel, out_shape=(codes, codes, codes, codes, pltpu.VMEM(...  124 us
    pallas_call x1, Pallas kernels, per_device(): pl.pallas_call(store_kernel, out_shape=(shape((2048, 1664), BF16), shape(...  5 us
  transfers between devices with their start and end apart: 1, of which 1 were waited for; matrix products, arithmetic and copies ran while one was open for 0% of the time, Pallas kernels for 4%

profile of v7, /device:TPU:0, one launch (start us, length us, event | category | flops | bytes accessed | tf_op | source)
XLA Modules:
  0.0 131.7 jit_solution(13168522431705391565)
XLA Ops:
  0.6 123.9 %shard_map.127 = (bf16[1024,1664]{1,0:T(8,128)(2,1)S(1)}, bf16[1024,1664]{1,0:T(8,128)(2,1)S(1)}, bf16[1024,1664]{1,0:T(8,128)(2,1)S(1)}, bf16[1024,1664]{1,0:T(...) custom-call(bf16[128,2048]{1,0:T(8,128)(2,1)} %bitcast.3, bf16[512,1664]{1,0:T(8,128)(2,1)} %bitcast.2, ...), custom_call_target="tpu_custom_call" | custom-call | flops 13958643712 | bytes 27262976 | tf_op jit(solution)/shard_map/pallas_call | solution.py:385
  124.6 0.8 collective-permute-start
  125.3 5.0 %shard_map.128 = (bf16[2048,1664]{1,0:T(8,128)(2,1)}, f32[16,13]{1,0:T(8,128)}, bf16[1024,1664]{1,0:T(8,128)(2,1)}, f32[8,13]{1,0:T(8,128)}, bf16[1024,1664]{1,0:T(8,128)(2,1)}, /*index=5*/f32[8,13]{1,0:T(8,128)}) custom-call(bf16[1024,1664]{1,0:T(8,128)(2,1)S(1)} %get-tuple-element.18.W, bf16[1024,1664]{1,0:T(8,128)(2,1)S(1)} %get-tuple-element.19.peer_w, ...), custom_call_target="tpu_custom_call" | custom-call | bytes 27262976 | tf_op jit(solution)/shard_map/pallas_call | solution.py:418
  130.3 0.7 collective-permute-done.peer_last
  131.0 0.7 shard_map.129
Async XLA Ops:
  124.6 6.5 %collective-permute-start = (bf16[1024,128]{1,0:T(8,128)(2,1)S(1)}, bf16[1024,128]{1,0:T(8,128)(2,1)S(1)}, u32[]{:S(2)}, u32[]{:S(2)}) collective-permute-start(bf16[1024,128]{1,0:T(8,128)(2,1)S(1)} %get-tuple-element.24), channel_id=1, source_target_pairs={{0,1},{1,0},{2,3},{3,2},{4,5},{5,4},{6,7},{7,6},{8,9},{9,8},{10,11... | collective-permute-start | bytes 786440 | tf_op jit(solution)/shard_map/ppermute | solution.py:417

commit v8 on v7

--- a/solution.py
+++ b/solution.py
@@ -207,7 +207,7 @@
         zf_landed(i).wait_recv()
         sib_copy(i, 3).start()
 
-    for i in (1, 2, 3):
+    for i in (1, 3, 2):
         y_copy(i).start()
     own = G.at[:, own_rows(p, c)]
     pltpu.make_async_copy(own, own, own_sem.at[0]).wait()

time: 132 us -> 132 us (level)
  no operation moved by 1% of the time
where the time goes in v8:
time: 132 us
  Pallas kernels  130 us (98%)
    pallas_call x1, Pallas kernels, per_device(): pl.pallas_call(kernel, out_shape=(codes, codes, codes, codes, pltpu.VMEM(...  124 us
    pallas_call x1, Pallas kernels, per_device(): pl.pallas_call(store_kernel, out_shape=(shape((2048, 1664), BF16), shape(...  5 us
  transfers between devices with their start and end apart: 1, of which 1 were waited for; matrix products, arithmetic and copies ran while one was open for 0% of the time, Pallas kernels for 4%

profile of v8, /device:TPU:0, one launch (start us, length us, event | category | flops | bytes accessed | tf_op | source)
XLA Modules:
  0.0 131.7 jit_solution(10772491751028410256)
XLA Ops:
  0.6 123.9 %shard_map.127 = (bf16[1024,1664]{1,0:T(8,128)(2,1)S(1)}, bf16[1024,1664]{1,0:T(8,128)(2,1)S(1)}, bf16[1024,1664]{1,0:T(8,128)(2,1)S(1)}, bf16[1024,1664]{1,0:T(...) custom-call(bf16[128,2048]{1,0:T(8,128)(2,1)} %bitcast.3, bf16[512,1664]{1,0:T(8,128)(2,1)} %bitcast.2, ...), custom_call_target="tpu_custom_call" | custom-call | flops 13958643712 | bytes 27262976 | tf_op jit(solution)/shard_map/pallas_call | solution.py:385
  124.6 0.8 collective-permute-start
  125.3 5.0 %shard_map.128 = (bf16[2048,1664]{1,0:T(8,128)(2,1)}, f32[16,13]{1,0:T(8,128)}, bf16[1024,1664]{1,0:T(8,128)(2,1)}, f32[8,13]{1,0:T(8,128)}, bf16[1024,1664]{1,0:T(8,128)(2,1)}, /*index=5*/f32[8,13]{1,0:T(8,128)}) custom-call(bf16[1024,1664]{1,0:T(8,128)(2,1)S(1)} %get-tuple-element.18.W, bf16[1024,1664]{1,0:T(8,128)(2,1)S(1)} %get-tuple-element.19.peer_w, ...), custom_call_target="tpu_custom_call" | custom-call | bytes 27262976 | tf_op jit(solution)/shard_map/pallas_call | solution.py:418
  130.3 0.7 collective-permute-done.peer_last
  131.0 0.7 shard_map.129
Async XLA Ops:
  124.6 6.5 %collective-permute-start = (bf16[1024,128]{1,0:T(8,128)(2,1)S(1)}, bf16[1024,128]{1,0:T(8,128)(2,1)S(1)}, u32[]{:S(2)}, u32[]{:S(2)}) collective-permute-start(bf16[1024,128]{1,0:T(8,128)(2,1)S(1)} %get-tuple-element.24), channel_id=1, source_target_pairs={{0,1},{1,0},{2,3},{3,2},{4,5},{5,4},{6,7},{7,6},{8,9},{9,8},{10,11... | collective-permute-start | bytes 786440 | tf_op jit(solution)/shard_map/ppermute | solution.py:417
